TPU v7x, 512 devices: a whole 4x4x16 slice. The times are simulated.
512 devices in a mesh: dist: 4 (over y_hi, core), tile: 128 (over y_lo, x, z).
Axes of the slice: x: 4, y: 4 (y_hi: 2, y_lo: 2; y = y_hi * 2 + y_lo), z: 16, core: 2. Of those that a mesh axis runs over, the one named last changes fastest.
Arguments:
- object_re: float32 [16384, 128], P('tile'), may hold values from -6 to 6
- object_im: float32 [16384, 128], P('tile'), may hold values from -6 to 6
- intensity: float32 [4, 16384, 128], P('dist', 'tile'), may hold values from 0.25 to 4
- shrink: int32 [4], P('dist'), may hold values from 32 to 64, as said below
- offset: int32 [4], P('dist'), may hold values from -31 to 31, as said below
- fresnel: int32 [4], P('dist'), may hold values from 4 to 16
Outputs:
- gradient_re: float32 [16384, 128], P('tile')
- gradient_im: float32 [16384, 128], P('tile')
Inputs may be any that keep to these rules, and one draw needn't show every extreme that they name: `shrink`: some distance has the largest value; the distances that take the two extreme offsets have the smallest. `offset`: both extreme values occur, at two different distances.
All inputs are finite; a program needn't handle non-finite values.
Results may differ from a plain program's by a relative error of at most 0.0003.
Values sent between devices are 32-bit elements; how exact they have to be, the bound alone decides.
No kernel may reach another device: no remote copies, remote signals or barrier semaphores. Data moves between devices by JAX's collectives and lax.ppermute only.
A program may use at most 128 MiB of HBM per device.

v0:
```python
from functools import partial
import math

import jax
import jax.numpy as jnp
from jax import lax
from jax.sharding import PartitionSpec as P

HIGHEST = lax.Precision.HIGHEST


def padded(cells, sides, width):
    for axis, dim in sides:
        count = lax.axis_size(axis)
        ends = count - 1
        head = lax.slice_in_dim(cells, 0, width, axis=dim)
        tail = lax.slice_in_dim(cells, cells.shape[dim] - width, cells.shape[dim], axis=dim)
        cells = jnp.concatenate(
            [
                lax.ppermute(tail, axis, [(i, (i + 1) % count) for i in range(ends)]),
                cells,
                lax.ppermute(head, axis, [((i + 1) % count, i) for i in range(ends)]),
            ],
            axis=dim,
        )
    return cells


def passed_along(value, axis, steps):
    count = lax.axis_size(axis)
    leading, last = (max(0, -steps), min(count, count - steps))
    return lax.ppermute(value, axis, [(source, source + steps) for source in range(leading, last)])


def angle_table(left_index, right_index, period):
    product = left_index[:, None] * right_index[None, :] % period
    theta = 2.0 * math.pi / period * product.astype(jnp.float32)
    return (jnp.cos(theta), -jnp.sin(theta))


def fresnel_kernel(frequency, fresnel_now, row_total):
    period = 64 * row_total
    signed = jnp.where(frequency < row_total // 2, frequency, frequency - row_total)
    square = signed * signed % period
    turns = fresnel_now * square % period
    theta = 2.0 * math.pi / period * turns.astype(jnp.float32)
    return (jnp.cos(theta), -jnp.sin(theta))


def complex_scale(values, factor):
    return (
        factor[0] * values[0] - factor[1] * values[1],
        factor[0] * values[1] + factor[1] * values[0],
    )


def table_apply(table, values, sign):
    real_table = table[0]
    imag_table = sign * table[1]
    shape = values[0].shape
    first_flat = values[0].reshape(shape[0], -1)
    second_flat = values[1].reshape(shape[0], -1)
    product = partial(jnp.dot, precision=HIGHEST, preferred_element_type=jnp.float32)
    out_real = product(real_table, first_flat) - product(imag_table, second_flat)
    out_imag = product(real_table, second_flat) + product(imag_table, first_flat)
    leading = (real_table.shape[0],) + shape[1:]
    return (out_real.reshape(leading), out_imag.reshape(leading))


def sample_rows(shrink_now, offset_now, first_row, count, row_total):
    centre = row_total // 2
    indices = first_row + jnp.arange(count, dtype=jnp.int32)
    scaled = (
        centre * row_total + (indices - centre) * (row_total - shrink_now) + offset_now * row_total
    )
    lower = jnp.floor_divide(scaled, row_total)
    weight = jnp.remainder(scaled, row_total).astype(jnp.float32) / row_total
    return (lower, weight)


def amplitude_residual(values, amplitude):
    magnitude = jnp.sqrt(values[0] * values[0] + values[1] * values[1])
    ratio = amplitude / jnp.maximum(magnitude, 0.1)
    return (values[0] - ratio * values[0], values[1] - ratio * values[1])


def exchange_blocks(values, tile_count):
    first_part = values[0].reshape(tile_count, -1, values[0].shape[-1])
    second_part = values[1].reshape(tile_count, -1, values[1].shape[-1])
    moved_real, moved_imag = (
        lax.all_to_all(first_part, "tile", split_axis=0, concat_axis=0, tiled=True),
        lax.all_to_all(second_part, "tile", split_axis=0, concat_axis=0, tiled=True),
    )
    return (moved_real, moved_imag)


def propagate_rows(values, outer_table, inner_table, twiddle, kernel, tile_count):
    row_count, col_count = values[0].shape
    spread = exchange_blocks(values, tile_count)
    mixed = table_apply(outer_table, spread, 1.0)
    mixed = complex_scale(mixed, (twiddle[0][:, :, None], twiddle[1][:, :, None]))
    gathered = exchange_blocks(mixed, tile_count)
    column_form = (
        gathered[0].reshape(row_count, col_count),
        gathered[1].reshape(row_count, col_count),
    )
    spectrum = table_apply(inner_table, column_form, 1.0)
    spectrum = complex_scale(spectrum, (kernel[0][:, None], kernel[1][:, None]))
    mixed = table_apply(inner_table, spectrum, -1.0)
    spread = exchange_blocks(mixed, tile_count)
    spread = complex_scale(spread, (twiddle[0][:, :, None], -twiddle[1][:, :, None]))
    mixed = table_apply(outer_table, spread, -1.0)
    returned = exchange_blocks(mixed, tile_count)
    factor = 1.0 / (row_count * tile_count)
    return (
        returned[0].reshape(row_count, col_count) * factor,
        returned[1].reshape(row_count, col_count) * factor,
    )


def body(object_re, object_im, intensity, shrink, offset, fresnel):
    row_count, col_count = object_re.shape
    tile_count = lax.axis_size("tile")
    row_total = row_count * tile_count
    halo_rows = row_count // 2
    tile_index = lax.axis_index("tile")
    shrink_now = shrink[0]
    offset_now = offset[0]
    fresnel_now = fresnel[0]
    tile_range = jnp.arange(tile_count, dtype=jnp.int32)
    row_range = jnp.arange(row_count, dtype=jnp.int32)
    outer_table = angle_table(tile_range, tile_range, tile_count)
    inner_table = angle_table(row_range, row_range, row_count)
    block_rows = row_count // tile_count
    amplitude = jnp.sqrt(intensity[0])
    first_row = tile_index * row_count
    mine = tile_index * block_rows + jnp.arange(block_rows, dtype=jnp.int32)
    twiddle = angle_table(tile_range, mine, row_total)
    frequency = tile_index + tile_count * row_range
    kernel = fresnel_kernel(frequency, fresnel_now, row_total)
    lower, weight = sample_rows(shrink_now, offset_now, first_row, row_count, row_total)
    slot = lower - first_row + halo_rows
    positions = jnp.arange(row_count + 2 * halo_rows, dtype=jnp.int32)
    below = jnp.where(positions[None, :] == slot[:, None], 1.0 - weight[:, None], 0.0)
    above = jnp.where(positions[None, :] == slot[:, None] + 1, weight[:, None], 0.0)
    sampling = below + above
    stacked = jnp.stack([object_re, object_im])
    extended = padded(stacked, (("tile", 1),), halo_rows)
    sampled = jnp.einsum(
        "rs,psc->prc", sampling, extended, precision=HIGHEST, preferred_element_type=jnp.float32
    )
    wave = propagate_rows(
        (sampled[0], sampled[1]), outer_table, inner_table, twiddle, kernel, tile_count
    )
    residual = amplitude_residual(wave, amplitude)
    back_wave = propagate_rows(
        residual, outer_table, inner_table, twiddle, (kernel[0], -kernel[1]), tile_count
    )
    spread = jnp.einsum(
        "rs,prc->psc",
        sampling,
        jnp.stack(back_wave),
        precision=HIGHEST,
        preferred_element_type=jnp.float32,
    )
    upper_rim = spread[:, :halo_rows]
    lower_rim = spread[:, row_count + halo_rows :]
    middle = spread[:, halo_rows : row_count + halo_rows]
    from_next = passed_along(upper_rim, "tile", -1)
    from_previous = passed_along(lower_rim, "tile", 1)
    own_terms = jnp.concatenate(
        [middle[:, :halo_rows] + from_previous, middle[:, halo_rows:] + from_next], axis=1
    )
    summed = lax.psum(own_terms, "dist")
    return (summed[0], summed[1])


def solution(mesh):
    in_specs = (
        P("tile", None),
        P("tile", None),
        P("dist", "tile", None),
        P("dist"),
        P("dist"),
        P("dist"),
    )
    out_specs = (P("tile", None), P("tile", None))
    return jax.shard_map(body, mesh=mesh, in_specs=in_specs, out_specs=out_specs, check_vma=False)
```

profile of v0, /device:TPU:1, one launch (start us, length us, event | category | flops | bytes accessed | tf_op | source)
XLA Modules:
  0.0 468.3 jit_solution(3767237596831190730)
XLA Ops:
  19.9 20.2 %all-to-all-start.1 = ((f32[128,1,128]{2,1,0:T(1,128)}), f32[128,1,128]{2,1,0:T(1,128)S(1)}, u32[]{:S(2)}, u32[]{:S(2)}) async-start(f32[128,1,128]{2,1,0:T(1,128)} %copy.16), calls=%async_computation.1 | async-start | bytes 131072 | tf_op jit(solution)/shard_map/all_to_all | solution.py:92
  40.8 13.3 %all-to-all-done.1 = f32[128,1,128]{2,1,0:T(1,128)S(1)} async-done(((f32[128,1,128]{2,1,0:T(1,128)}), f32[128,1,128]{2,1,0:T(1,128)S(1)}, u32[]{:S(2)}, u32[]{:S(2)}) %all-to-all-start.1) | async-done | bytes 65568 | tf_op jit(solution)/shard_map/all_to_all | solution.py:92
  60.8 13.5 %all-to-all-done = f32[128,1,128]{2,1,0:T(1,128)S(1)} async-done(((f32[128,1,128]{2,1,0:T(1,128)}), f32[128,1,128]{2,1,0:T(1,128)S(1)}, u32[]{:S(2)}, u32[]{:S(2)}) %all-to-all-start) | async-done | bytes 65568 | tf_op jit(solution)/shard_map/all_to_all | solution.py:91
  83.2 13.4 %all-to-all-done.2 = f32[128,1,128]{2,1,0:T(1,128)S(1)} async-done(((f32[128,1,128]{2,1,0:T(1,128)}), f32[128,1,128]{2,1,0:T(1,128)S(1)}, u32[]{:S(2)}, u32[]{:S(2)}) %all-to-all-start.2) | async-done | bytes 65568 | tf_op jit(solution)/shard_map/all_to_all | solution.py:91
  96.6 6.6 %all-to-all-start.3 = ((f32[128,1,128]{2,1,0:T(1,128)}), f32[128,1,128]{2,1,0:T(1,128)S(1)}, u32[]{:S(2)}, u32[]{:S(2)}) async-start(f32[128,1,128]{2,1,0:T(1,128)} %bitcast.15), calls=%async_computation.3 | async-start | bytes 131072 | tf_op jit(solution)/shard_map/all_to_all | solution.py:92
  103.7 13.5 %all-to-all-done.3 = f32[128,1,128]{2,1,0:T(1,128)S(1)} async-done(((f32[128,1,128]{2,1,0:T(1,128)}), f32[128,1,128]{2,1,0:T(1,128)S(1)}, u32[]{:S(2)}, u32[]{:S(2)}) %all-to-all-start.3) | async-done | bytes 65568 | tf_op jit(solution)/shard_map/all_to_all | solution.py:92
  127.9 12.5 %all-to-all-done.5 = f32[128,1,128]{2,1,0:T(1,128)S(1)} async-done(((f32[128,1,128]{2,1,0:T(1,128)}), f32[128,1,128]{2,1,0:T(1,128)S(1)}, u32[]{:S(2)}, u32[]{:S(2)}) %all-to-all-start.5) | async-done | bytes 65568 | tf_op jit(solution)/shard_map/all_to_all | solution.py:92
  146.6 14.0 %all-to-all-done.4 = f32[128,1,128]{2,1,0:T(1,128)S(1)} async-done(((f32[128,1,128]{2,1,0:T(1,128)}), f32[128,1,128]{2,1,0:T(1,128)S(1)}, u32[]{:S(2)}, u32[]{:S(2)}) %all-to-all-start.4) | async-done | bytes 65568 | tf_op jit(solution)/shard_map/all_to_all | solution.py:91
  170.1 12.5 %all-to-all-done.7 = f32[128,1,128]{2,1,0:T(1,128)S(1)} async-done(((f32[128,1,128]{2,1,0:T(1,128)}), f32[128,1,128]{2,1,0:T(1,128)S(1)}, u32[]{:S(2)}, u32[]{:S(2)}) %all-to-all-start.7) | async-done | bytes 65568 | tf_op jit(solution)/shard_map/all_to_all | solution.py:92
  182.7 6.5 %all-to-all-start.6 = ((f32[128,1,128]{2,1,0:T(1,128)}), f32[128,1,128]{2,1,0:T(1,128)S(1)}, u32[]{:S(2)}, u32[]{:S(2)}) async-start(f32[128,1,128]{2,1,0:T(1,128)} %bitcast.24), calls=%async_computation.6 | async-start | bytes 131072 | tf_op jit(solution)/shard_map/all_to_all | solution.py:91
  189.3 13.8 %all-to-all-done.6 = f32[128,1,128]{2,1,0:T(1,128)S(1)} async-done(((f32[128,1,128]{2,1,0:T(1,128)}), f32[128,1,128]{2,1,0:T(1,128)S(1)}, u32[]{:S(2)}, u32[]{:S(2)}) %all-to-all-start.6) | async-done | bytes 65568 | tf_op jit(solution)/shard_map/all_to_all | solution.py:91
  210.9 13.3 %all-to-all-done.9 = f32[128,1,128]{2,1,0:T(1,128)S(1)} async-done(((f32[128,1,128]{2,1,0:T(1,128)}), f32[128,1,128]{2,1,0:T(1,128)S(1)}, u32[]{:S(2)}, u32[]{:S(2)}) %all-to-all-start.9) | async-done | bytes 65568 | tf_op jit(solution)/shard_map/all_to_all | solution.py:92
  224.3 6.1 %all-to-all-start.8 = ((f32[128,1,128]{2,1,0:T(1,128)}), f32[128,1,128]{2,1,0:T(1,128)S(1)}, u32[]{:S(2)}, u32[]{:S(2)}) async-start(f32[128,1,128]{2,1,0:T(1,128)} %copy.26), calls=%async_computation.8 | async-start | bytes 131072 | tf_op jit(solution)/shard_map/all_to_all | solution.py:91
  230.9 13.6 %all-to-all-done.8 = f32[128,1,128]{2,1,0:T(1,128)S(1)} async-done(((f32[128,1,128]{2,1,0:T(1,128)}), f32[128,1,128]{2,1,0:T(1,128)S(1)}, u32[]{:S(2)}, u32[]{:S(2)}) %all-to-all-start.8) | async-done | bytes 65568 | tf_op jit(solution)/shard_map/all_to_all | solution.py:91
  246.5 19.6 %all_to_all.80 = f32[128,1,128]{2,1,0:T(1,128)S(1)} all-to-all(f32[128,1,128]{2,1,0:T(1,128)S(1)} %bitcast.126), channel_id=1, replica_groups=mesh['dist'=4,'tile'=128] {'tile'}, dimensions={0} | all-to-all | bytes 131072 | tf_op jit(solution)/shard_map/all_to_all | solution.py:91
  266.1 6.4 %all-to-all-start.11 = ((f32[128,1,128]{2,1,0:T(1,128)}), f32[128,1,128]{2,1,0:T(1,128)S(1)}, u32[]{:S(2)}, u32[]{:S(2)}) async-start(f32[128,1,128]{2,1,0:T(1,128)} %bitcast.34), calls=%async_computation.11 | async-start | bytes 131072 | tf_op jit(solution)/shard_map/all_to_all | solution.py:92
  272.9 13.6 %all-to-all-done.11 = f32[128,1,128]{2,1,0:T(1,128)S(1)} async-done(((f32[128,1,128]{2,1,0:T(1,128)}), f32[128,1,128]{2,1,0:T(1,128)S(1)}, u32[]{:S(2)}, u32[]{:S(2)}) %all-to-all-start.11) | async-done | bytes 65568 | tf_op jit(solution)/shard_map/all_to_all | solution.py:92
  289.5 6.2 %all-to-all-start.13 = ((f32[128,1,128]{2,1,0:T(1,128)}), f32[128,1,128]{2,1,0:T(1,128)S(1)}, u32[]{:S(2)}, u32[]{:S(2)}) async-start(f32[128,1,128]{2,1,0:T(1,128)} %bitcast.39), calls=%async_computation.13 | async-start | bytes 131072 | tf_op jit(solution)/shard_map/all_to_all | solution.py:92
  296.5 13.1 %all-to-all-done.13 = f32[128,1,128]{2,1,0:T(1,128)S(1)} async-done(((f32[128,1,128]{2,1,0:T(1,128)}), f32[128,1,128]{2,1,0:T(1,128)S(1)}, u32[]{:S(2)}, u32[]{:S(2)}) %all-to-all-start.13) | async-done | bytes 65568 | tf_op jit(solution)/shard_map/all_to_all | solution.py:92
  309.7 19.7 %all_to_all.81 = f32[128,1,128]{2,1,0:T(1,128)S(1)} all-to-all(f32[128,1,128]{2,1,0:T(1,128)S(1)} %bitcast.125), channel_id=1, replica_groups=mesh['dist'=4,'tile'=128] {'tile'}, dimensions={0} | all-to-all | bytes 131072 | tf_op jit(solution)/shard_map/all_to_all | solution.py:91
  331.2 6.1 %all-to-all-start.15 = ((f32[128,1,128]{2,1,0:T(1,128)}), f32[128,1,128]{2,1,0:T(1,128)S(1)}, u32[]{:S(2)}, u32[]{:S(2)}) async-start(f32[128,1,128]{2,1,0:T(1,128)} %bitcast.46), calls=%async_computation.15 | async-start | bytes 131072 | tf_op jit(solution)/shard_map/all_to_all | solution.py:92
  338.9 12.5 %all-to-all-done.15 = f32[128,1,128]{2,1,0:T(1,128)S(1)} async-done(((f32[128,1,128]{2,1,0:T(1,128)}), f32[128,1,128]{2,1,0:T(1,128)S(1)}, u32[]{:S(2)}, u32[]{:S(2)}) %all-to-all-start.15) | async-done | bytes 65568 | tf_op jit(solution)/shard_map/all_to_all | solution.py:92
  357.8 13.9 %all-to-all-done.14 = f32[128,1,128]{2,1,0:T(1,128)S(1)} async-done(((f32[128,1,128]{2,1,0:T(1,128)}), f32[128,1,128]{2,1,0:T(1,128)S(1)}, u32[]{:S(2)}, u32[]{:S(2)}) %all-to-all-start.14) | async-done | bytes 65568 | tf_op jit(solution)/shard_map/all_to_all | solution.py:91
  384.2 74.6 %all-reduce.2.cloned.1.call-done = f32[2,128,128]{1,2,0:T(8,128)} async-done(((f32[2,128,128]{1,2,0:T(8,128)}), f32[2,128,128]{1,2,0:T(8,128)}) %all-reduce.2.cloned.1.call-update) | async-done | bytes 131088 | tf_op jit(solution)/shard_map/psum | solution.py:174
  (85 shorter events, 93.0 us)
Async XLA Ops:
  7.2 1.0 copy-start
  8.3 7.0 %collective-permute-start = (f32[2,64,128]{1,2,0:T(8,128)S(1)}, f32[2,64,128]{1,2,0:T(8,128)S(1)}, u32[]{:S(2)}, u32[]{:S(2)}) collective-permute-start(f32[2,64,128]{1,2,0:T(8,128)S(1)} %get-tuple-element.26), channel_id=1, source_target_pairs={{0,1},{1,2},{2,3},{3,4},{4,5},{5,6},{6,7},{7,8},{8,9},{9,10},{10,1... | collective-permute-start | bytes 196616 | tf_op jit(solution)/shard_map/ppermute | solution.py:20
  12.7 5.9 %collective-permute-start.1 = (f32[2,64,128]{1,2,0:T(8,128)S(1)}, f32[2,64,128]{1,2,0:T(8,128)S(1)}, u32[]{:S(2)}, u32[]{:S(2)}) collective-permute-start(f32[2,64,128]{1,2,0:T(8,128)S(1)} %get-tuple-element.27), channel_id=1, source_target_pairs={{1,0},{2,1},{3,2},{4,3},{5,4},{6,5},{7,6},{8,7},{9,8},{10,9},{11,1... | collective-permute-start | bytes 196616 | tf_op jit(solution)/shard_map/ppermute | solution.py:22
  19.9 34.2 %all-to-all-start.1 = ((f32[128,1,128]{2,1,0:T(1,128)}), f32[128,1,128]{2,1,0:T(1,128)S(1)}, u32[]{:S(2)}, u32[]{:S(2)}) async-start(f32[128,1,128]{2,1,0:T(1,128)} %copy.16), calls=%async_computation.1 | async-start | bytes 131072 | tf_op jit(solution)/shard_map/all_to_all | solution.py:92
  54.1 20.2 %all-to-all-start = ((f32[128,1,128]{2,1,0:T(1,128)}), f32[128,1,128]{2,1,0:T(1,128)S(1)}, u32[]{:S(2)}, u32[]{:S(2)}) async-start(f32[128,1,128]{2,1,0:T(1,128)} %copy.15), calls=%async_computation | async-start | bytes 131072 | tf_op jit(solution)/shard_map/all_to_all | solution.py:91
  76.4 20.2 %all-to-all-start.2 = ((f32[128,1,128]{2,1,0:T(1,128)}), f32[128,1,128]{2,1,0:T(1,128)S(1)}, u32[]{:S(2)}, u32[]{:S(2)}) async-start(f32[128,1,128]{2,1,0:T(1,128)} %bitcast.12), calls=%async_computation.2 | async-start | bytes 131072 | tf_op jit(solution)/shard_map/all_to_all | solution.py:91
  96.6 20.7 %all-to-all-start.3 = ((f32[128,1,128]{2,1,0:T(1,128)}), f32[128,1,128]{2,1,0:T(1,128)S(1)}, u32[]{:S(2)}, u32[]{:S(2)}) async-start(f32[128,1,128]{2,1,0:T(1,128)} %bitcast.15), calls=%async_computation.3 | async-start | bytes 131072 | tf_op jit(solution)/shard_map/all_to_all | solution.py:92
  120.2 20.2 %all-to-all-start.5 = ((f32[128,1,128]{2,1,0:T(1,128)}), f32[128,1,128]{2,1,0:T(1,128)S(1)}, u32[]{:S(2)}, u32[]{:S(2)}) async-start(f32[128,1,128]{2,1,0:T(1,128)} %bitcast.20), calls=%async_computation.5 | async-start | bytes 131072 | tf_op jit(solution)/shard_map/all_to_all | solution.py:92
  140.4 20.2 %all-to-all-start.4 = ((f32[128,1,128]{2,1,0:T(1,128)}), f32[128,1,128]{2,1,0:T(1,128)S(1)}, u32[]{:S(2)}, u32[]{:S(2)}) async-start(f32[128,1,128]{2,1,0:T(1,128)} %bitcast.18), calls=%async_computation.4 | async-start | bytes 131072 | tf_op jit(solution)/shard_map/all_to_all | solution.py:91
  162.5 20.2 %all-to-all-start.7 = ((f32[128,1,128]{2,1,0:T(1,128)}), f32[128,1,128]{2,1,0:T(1,128)S(1)}, u32[]{:S(2)}, u32[]{:S(2)}) async-start(f32[128,1,128]{2,1,0:T(1,128)} %bitcast.27), calls=%async_computation.7 | async-start | bytes 131072 | tf_op jit(solution)/shard_map/all_to_all | solution.py:92
  182.7 6.5 %copy-start.1 = (f32[1,128,128]{2,1,0:T(8,128)S(1)}, f32[1,128,128]{2,1,0:T(8,128)}, u32[]{:S(2)}) copy-start(f32[1,128,128]{2,1,0:T(8,128)} %param.8) | copy-start | bytes 196612
  182.7 20.5 %all-to-all-start.6 = ((f32[128,1,128]{2,1,0:T(1,128)}), f32[128,1,128]{2,1,0:T(1,128)S(1)}, u32[]{:S(2)}, u32[]{:S(2)}) async-start(f32[128,1,128]{2,1,0:T(1,128)} %bitcast.24), calls=%async_computation.6 | async-start | bytes 131072 | tf_op jit(solution)/shard_map/all_to_all | solution.py:91
  204.1 20.2 %all-to-all-start.9 = ((f32[128,1,128]{2,1,0:T(1,128)}), f32[128,1,128]{2,1,0:T(1,128)S(1)}, u32[]{:S(2)}, u32[]{:S(2)}) async-start(f32[128,1,128]{2,1,0:T(1,128)} %copy.27), calls=%async_computation.9 | async-start | bytes 131072 | tf_op jit(solution)/shard_map/all_to_all | solution.py:92
  224.3 20.2 %all-to-all-start.8 = ((f32[128,1,128]{2,1,0:T(1,128)}), f32[128,1,128]{2,1,0:T(1,128)S(1)}, u32[]{:S(2)}, u32[]{:S(2)}) async-start(f32[128,1,128]{2,1,0:T(1,128)} %copy.26), calls=%async_computation.8 | async-start | bytes 131072 | tf_op jit(solution)/shard_map/all_to_all | solution.py:91
  266.1 20.4 %all-to-all-start.11 = ((f32[128,1,128]{2,1,0:T(1,128)}), f32[128,1,128]{2,1,0:T(1,128)S(1)}, u32[]{:S(2)}, u32[]{:S(2)}) async-start(f32[128,1,128]{2,1,0:T(1,128)} %bitcast.34), calls=%async_computation.11 | async-start | bytes 131072 | tf_op jit(solution)/shard_map/all_to_all | solution.py:92
  289.5 20.2 %all-to-all-start.13 = ((f32[128,1,128]{2,1,0:T(1,128)}), f32[128,1,128]{2,1,0:T(1,128)S(1)}, u32[]{:S(2)}, u32[]{:S(2)}) async-start(f32[128,1,128]{2,1,0:T(1,128)} %bitcast.39), calls=%async_computation.13 | async-start | bytes 131072 | tf_op jit(solution)/shard_map/all_to_all | solution.py:92
  331.2 20.2 %all-to-all-start.15 = ((f32[128,1,128]{2,1,0:T(1,128)}), f32[128,1,128]{2,1,0:T(1,128)S(1)}, u32[]{:S(2)}, u32[]{:S(2)}) async-start(f32[128,1,128]{2,1,0:T(1,128)} %bitcast.46), calls=%async_computation.15 | async-start | bytes 131072 | tf_op jit(solution)/shard_map/all_to_all | solution.py:92
  351.5 20.3 %all-to-all-start.14 = ((f32[128,1,128]{2,1,0:T(1,128)}), f32[128,1,128]{2,1,0:T(1,128)S(1)}, u32[]{:S(2)}, u32[]{:S(2)}) async-start(f32[128,1,128]{2,1,0:T(1,128)} %bitcast.43), calls=%async_computation.14 | async-start | bytes 131072 | tf_op jit(solution)/shard_map/all_to_all | solution.py:91
  357.6 101.2 %all-reduce.2.cloned.1.call-start = ((), (), s32[]{:S(2)}) async-start(), calls=%async_computation.16 | async-start | bytes 262144 | tf_op jit(solution)/shard_map/psum | solution.py:174
  372.4 4.3 collective-permute-start.2
  376.8 6.6 %collective-permute-start.3 = (f32[2,64,128]{1,2,0:T(8,128)S(1)}, f32[2,64,128]{1,2,0:T(8,128)S(1)}, u32[]{:S(2)}, u32[]{:S(2)}) collective-permute-start(f32[2,64,128]{1,2,0:T(8,128)S(1)} %get-tuple-element.11), channel_id=1, source_target_pairs={{1,0},{2,1},{3,2},{4,3},{5,4},{6,5},{7,6},{8,7},{9,8},{10,9},{11,1... | collective-permute-start | bytes 196616 | tf_op jit(solution)/shard_map/ppermute | solution.py:32
Sparse Core Ops, SparseCore 0:
  384.3 74.4 all-reduce.1
where the time goes:
time: 477 us; the launch traced here: 468 us
  waiting for transfers between devices  272 us (57%)
  starting transfers between devices  110 us (23%)
  blocking collectives  39.3 us (8%)
  matrix products  21.3 us (4%)
  between operations  16.6 us (3%)
  local copies, waits for them, and re-layouts  6.86 us (1%)
    all_to_all x8, waiting for transfers between devices, exchange_blocks(): lax.all_to_all(second_part, 'tile', split_axis=0, concat_axis=0, tiled=True)  104 us
    all_to_all x6, waiting for transfers between devices, exchange_blocks(): lax.all_to_all(first_part, 'tile', split_axis=0, concat_axis=0, tiled=True)  82.3 us
    psum x1, waiting for transfers between devices, body(): summed = lax.psum(own_terms, 'dist')  74.6 us
    all_to_all x8, starting transfers between devices, exchange_blocks(): lax.all_to_all(second_part, 'tile', split_axis=0, concat_axis=0, tiled=True)  63.9 us
    all_to_all x2, blocking collectives, exchange_blocks(): lax.all_to_all(first_part, 'tile', split_axis=0, concat_axis=0, tiled=True)  39.3 us
    all_to_all x6, starting transfers between devices, exchange_blocks(): lax.all_to_all(first_part, 'tile', split_axis=0, concat_axis=0, tiled=True)  37.2 us
  transfers between devices with their start and end apart: 19, of which 18 were waited for; matrix products, arithmetic and copies ran while one was open for 2% of the time, Pallas kernels for 0%

commit v1 on v0

v1 whole, which is shorter than its diff:
```python
from functools import partial
import math

import jax
import jax.numpy as jnp
import numpy as np
from jax import lax
from jax.experimental import pallas as pl
from jax.experimental.pallas import tpu as pltpu
from jax.sharding import PartitionSpec as P

F32 = jnp.float32
BF16 = jnp.bfloat16


def two_terms(values):
    high = values.astype(BF16)
    low = (values - high.astype(np.float32)).astype(BF16)
    return high, low


def constant_tables(size):
    index = np.arange(size, dtype=np.int64)
    product = np.outer(index, index)
    angle = 2.0 * np.pi / size * (product % size)
    real, imag = np.cos(angle), -np.sin(angle)
    block = np.block([[real, -imag], [imag, real]]).astype(np.float32)
    angle = 2.0 * np.pi / (size * size) * product
    twiddle = np.stack([np.cos(angle), -np.sin(angle)]).astype(np.float32)
    return two_terms(block) + (twiddle,)


def split(values):
    high = values.astype(BF16)
    return high, (values - high.astype(F32)).astype(BF16)


def product(left, right):
    dot = partial(jnp.dot, preferred_element_type=F32)
    return dot(left[0], right[0]) + (dot(left[0], right[1]) + dot(left[1], right[0]))


def times(first, second):
    return (
        first[0] * second[0] - first[1] * second[1],
        first[0] * second[1] + first[1] * second[0],
    )


def conj(pair):
    return (pair[0], -pair[1])


def propagate(values, block, block_t, twiddle, kernel, size):
    def by_rows(table, pair):
        out = product(table, split(jnp.concatenate(pair, axis=0)))
        return (out[:size], out[size:])

    def by_lanes(pair, table):
        out = product(split(jnp.concatenate(pair, axis=1)), table)
        return (out[:, :size], out[:, size:])

    mixed = times(by_rows(block, values), twiddle)
    spectrum = times(by_lanes(mixed, block_t), kernel)
    mixed = times(by_lanes(spectrum, block), conj(twiddle))
    return by_rows(block_t, mixed)


def column_kernel(size, scalars, field_ref, phase_ref, high_ref, low_ref, high_t_ref, low_t_ref, twiddle_ref, out_ref):
    shape = (size, size)
    row = lax.broadcasted_iota(jnp.int32, shape, 0)
    lane = lax.broadcasted_iota(jnp.int32, shape, 1)
    total = size * size
    bits = total.bit_length() - 1
    shrink, offset = scalars[0], scalars[1]

    def scaled(index):
        centre = total // 2
        return centre * total + (index - centre) * (total - shrink) + offset * total

    place = scaled(row * size + lane)
    weight = jnp.bitwise_and(place, total - 1).astype(F32) * (1.0 / total)
    shift = lax.shift_right_arithmetic(scaled(row * size), bits) - row * size
    leading = lax.shift_right_arithmetic(place, bits) - (row * size + lane) == shift
    rest = 1.0 - weight

    def rows_up(values):
        moved = pltpu.roll(values, size - 1, 0)
        return jnp.where(row == size - 1, 0.0, moved)

    def rows_down(values):
        moved = pltpu.roll(values, 1, 0)
        return jnp.where(row == 0, 0.0, moved)

    def lanes(values, index):
        return jnp.take_along_axis(values, jnp.bitwise_and(index, size - 1), axis=1, mode="promise_in_bounds")

    def sample(values):
        below, above = rows_down(values), rows_up(values)

        def displaced(by):
            source = jnp.where(lane < by, above, jnp.where(lane >= by + size, below, values))
            return lanes(source, lane + by)

        centre = displaced(shift)
        return jnp.where(
            leading,
            rest * centre + weight * displaced(shift + 1),
            rest * displaced(shift - 1) + weight * centre,
        )

    def spread(values):
        near, far = rest * values, weight * values
        stay = up = down = 0.0
        for by, part in (
            (shift, jnp.where(leading, near, far)),
            (shift - 1, jnp.where(leading, 0.0, near)),
            (shift + 1, jnp.where(leading, far, 0.0)),
        ):
            moved = lanes(part, lane - by)
            to_next = lane < by
            to_last = lane >= by + size
            down += jnp.where(to_next, moved, 0.0)
            up += jnp.where(to_last, moved, 0.0)
            stay += jnp.where(jnp.logical_or(to_next, to_last), 0.0, moved)
        return stay + rows_down(down) + rows_up(up)

    block = (high_ref[...], low_ref[...])
    block_t = (high_t_ref[...], low_t_ref[...])
    twiddle = (twiddle_ref[0], twiddle_ref[1])
    kernel = (phase_ref[0], phase_ref[1])
    sampled = (sample(field_ref[:, :size]), sample(field_ref[:, size : 2 * size]))
    wave = propagate(sampled, block, block_t, twiddle, kernel, size)
    power = wave[0] * wave[0] + wave[1] * wave[1]
    kept = 1.0 - jnp.sqrt(field_ref[:, 2 * size :] / jnp.maximum(power, 0.01))
    residual = (kept * wave[0], kept * wave[1])
    back = propagate(residual, block, block_t, twiddle, conj(kernel), size)
    out_ref[:, :size] = spread(back[0])
    out_ref[:, size:] = spread(back[1])


def fresnel_phase(fresnel_now, size):
    total = size * size
    period = 64 * total
    index = jnp.arange(size, dtype=jnp.int32)
    frequency = index[:, None] + size * index[None, :]
    signed = jnp.where(frequency < total // 2, frequency, frequency - total)
    turns = fresnel_now * (signed * signed % period) % period
    theta = 2.0 * math.pi / period * turns.astype(F32)
    return jnp.stack([jnp.cos(theta), -jnp.sin(theta)]) * (1.0 / total)


def run_column(scalars, field, phase, size, **options):
    high, low, twiddle = constant_tables(size)
    vmem = pl.BlockSpec(memory_space=pltpu.VMEM)
    return pl.pallas_call(
        partial(column_kernel, size),
        out_shape=jax.ShapeDtypeStruct((size, 2 * size), F32),
        in_specs=[pl.BlockSpec(memory_space=pltpu.SMEM)] + [vmem] * 7,
        out_specs=vmem,
        compiler_params=pltpu.CompilerParams(vmem_limit_bytes=32 * 1024 * 1024),
        name="column",
        **options,
    )(
        scalars,
        field,
        phase,
        jnp.asarray(high),
        jnp.asarray(low),
        jnp.asarray(high.T),
        jnp.asarray(low.T),
        jnp.asarray(twiddle),
    )


def body(object_re, object_im, intensity, shrink, offset, fresnel):
    size = object_re.shape[0]
    tile_count = lax.axis_size("tile")
    phase = fresnel_phase(fresnel[0], size)
    columns = jnp.concatenate([object_re.T, object_im.T, intensity[0].T], axis=1)
    columns = columns.reshape(tile_count, 1, 3 * size)
    field = lax.all_to_all(columns, "tile", split_axis=0, concat_axis=0, tiled=True)
    field = field.reshape(tile_count, 3 * size)
    gradient = run_column(jnp.concatenate([shrink, offset]), field, phase, size)
    tiles = lax.all_to_all(
        gradient.reshape(tile_count, 1, 2 * size), "tile", split_axis=0, concat_axis=0, tiled=True
    ).reshape(tile_count, 2 * size)
    total = tiles.T
    for partner in (1, 2):
        pairs = [(i, i ^ partner) for i in range(lax.axis_size("dist"))]
        total = total + lax.ppermute(total, "dist", pairs)
    return (total[:size], total[size:])


def solution(mesh):
    in_specs = (
        P("tile", None),
        P("tile", None),
        P("dist", "tile", None),
        P("dist"),
        P("dist"),
        P("dist"),
    )
    out_specs = (P("tile", None), P("tile", None))
    return jax.shard_map(body, mesh=mesh, in_specs=in_specs, out_specs=out_specs, check_vma=False)
```

time: 477 us -> 85.4 us (0.18); the launches traced: 468 us -> 85.1 us
  waiting for transfers between devices: 272 us -> 18.9 us
  starting transfers between devices: 110 us -> 31.4 us
  matrix products: 21.3 us -> 0 us
  blocking collectives: 39.3 us -> 24.1 us
  between operations: 16.6 us -> 2.79 us
    all_to_all x14 -> x1, waiting for transfers between devices: 187 us -> 14.4 us  [body(): lax.all_to_all(columns, 'tile', split_axis=0, concat_axis=0, tiled=True)]
    all_to_all x14 -> x1, starting transfers between devices: 101 us -> 21.3 us  [body(): lax.all_to_all(columns, 'tile', split_axis=0, concat_axis=0, tiled=True)]
    psum x1 -> x0, waiting for transfers between devices: 74.6 us -> none  [body(): summed = lax.psum(own_terms, 'dist')]
    dot_general x34 -> x0, matrix products: 21.3 us -> none  [the longest x8 7.5 us: table_apply(): product(imag_table, first_flat)]
    all_to_all x2 -> x1, blocking collectives: 39.3 us -> 24.1 us  [body(): lax.all_to_all(gradient.reshape(tile_count, 1, 2 * size), 'tile', split_a...]
    ppermute x4 -> x2, waiting for transfers between devices: 10.4 us -> 4.55 us  [body(): total = total + lax.ppermute(total, 'dist', pairs)]
    ppermute x4 -> x2, starting transfers between devices: 9.35 us -> 10 us  [body(): total = total + lax.ppermute(total, 'dist', pairs)]
  transfers between devices with their start and end apart: 19 -> 3, of which waited for: 18 -> 3; matrix products, arithmetic and copies ran while one was open for 2% -> 0% of each run, Pallas kernels for 0% -> 0%
where the time goes in v1:
time: 85.4 us; the launch traced here: 85.1 us
  starting transfers between devices  31.4 us (37%)
  blocking collectives  24.1 us (28%)
  waiting for transfers between devices  18.9 us (22%)
  local copies, waits for them, and re-layouts  4.35 us (5%)
  Pallas kernels  3.05 us (4%)
  between operations  2.79 us (3%)
    all_to_all x1, blocking collectives, body(): lax.all_to_all(gradient.reshape(tile_count, 1, 2 * size), 'tile', split_a...  24.1 us
    all_to_all x1, starting transfers between devices, body(): lax.all_to_all(columns, 'tile', split_axis=0, concat_axis=0, tiled=True)  21.3 us
    all_to_all x1, waiting for transfers between devices, body(): lax.all_to_all(columns, 'tile', split_axis=0, concat_axis=0, tiled=True)  14.4 us
    ppermute x2, starting transfers between devices, body(): total = total + lax.ppermute(total, 'dist', pairs)  10 us
    ppermute x2, waiting for transfers between devices, body(): total = total + lax.ppermute(total, 'dist', pairs)  4.55 us
    unnamed x21, local copies, waits for them, and re-layouts  3.39 us
    pallas_call x1, Pallas kernels, run_column(): pl.pallas_call(partial(column_kernel, size), out_shape=jax.ShapeDtypeStru...  3.05 us
  transfers between devices with their start and end apart: 3, of which 3 were waited for; matrix products, arithmetic and copies ran while one was open for 0% of the time, Pallas kernels for 0%

profile of v1, /device:TPU:1, one launch (start us, length us, event | category | flops | bytes accessed | tf_op | source)
XLA Modules:
  0.0 85.1 jit_solution(15772934956007884293)
XLA Ops:
  0.6 1.0 %copy.18 = f32[128,128]{0,1:T(8,128)S(1)} copy(f32[128,128]{1,0:T(8,128)} %param.11) | data formatting | bytes 131072 | tf_op args[0]
  1.6 0.0 copy-start.6
  1.6 0.1 copy.19
  1.7 0.7 copy-done.6
  2.5 0.1 copy.20
  2.6 0.8 reshape.171
  3.4 21.3 %all-to-all-start = ((f32[128,1,384]{2,1,0:T(1,128)}), f32[128,1,384]{2,1,0:T(1,128)S(1)}, u32[]{:S(2)}, u32[]{:S(2)}) async-start(f32[128,1,384]{2,1,0:T(1,128)} %reshape.171), calls=%async_computation | async-start | bytes 393216 | tf_op jit(solution)/shard_map/all_to_all | solution.py:182
  26.7 0.1 pad_add_fusion.scalars
  26.8 0.3 fusion.6
  27.1 0.0 copy-start.3
  27.1 0.0 copy-start.4
  27.1 0.0 copy-start
  27.1 0.0 copy-start.1
  27.2 0.0 copy-start.2
  27.2 14.4 %all-to-all-done = f32[128,1,384]{2,1,0:T(1,128)S(1)} async-done(((f32[128,1,384]{2,1,0:T(1,128)}), f32[128,1,384]{2,1,0:T(1,128)S(1)}, u32[]{:S(2)}, u32[]{:S(2)}) %all-to-all-start) | async-done | bytes 196640 | tf_op jit(solution)/shard_map/all_to_all | solution.py:182
  41.6 3.0 %column.1 = f32[128,256]{1,0:T(8,128)S(1)} custom-call(s32[2]{0:T(128)S(1)} %pad_add_fusion.scalars, f32[128,384]{1,0:T(8,128)S(1)} %bitcast.18, f32[2,128,128]{2,1,0:T(8,128)S(1)} %maximum_multiply_fusion.phase_ref, bf16[256,256]{1,0:T(8,128)(2,1)S(1)} %copy-done.4, bf16[256,256]{1,0:T(8,128)(2,1)S(1)} %copy-done.3, bf16[256,256]{1,0:T(8,128)(2,1)S(1)} %copy-done.2, ...), custom_call_target="tpu_custom_call" | custom-call | tf_op jit(solution)/shard_map/column/pallas_call | solution.py:156
  44.7 0.1 copy.21
  44.8 24.1 %all_to_all.10 = f32[128,1,256]{2,1,0:T(1,128)S(1)} all-to-all(f32[128,1,256]{2,1,0:T(1,128)S(1)} %copy.21), channel_id=1, replica_groups=mesh['dist'=4,'tile'=128] {'tile'}, dimensions={0} | all-to-all | bytes 262144 | tf_op jit(solution)/shard_map/all_to_all | solution.py:185
  69.0 5.5 %collective-permute-start = (f32[256,128]{0,1:T(8,128)S(1)}, f32[256,128]{0,1:T(8,128)S(1)}, u32[]{:S(2)}, u32[]{:S(2)}) collective-permute-start(f32[256,128]{0,1:T(8,128)S(1)} %bitcast.23), channel_id=1, source_target_pairs={{0,128},{128,0},{256,384},{384,256},{1,129},{129,1},{257,385},{385... | collective-permute-start | bytes 393224 | tf_op jit(solution)/shard_map/ppermute | solution.py:191
  74.5 1.0 %collective-permute-done = f32[256,128]{0,1:T(8,128)S(1)} collective-permute-done((f32[256,128]{0,1:T(8,128)S(1)}, f32[256,128]{0,1:T(8,128)S(1)}, u32[]{:S(2)}, u32[]{:S(2)}) %collective-permute-start) | collective-permute-done | bytes 131104 | tf_op jit(solution)/shard_map/ppermute | solution.py:191
  75.5 4.5 %collective-permute-start.1 = (f32[256,128]{0,1:T(8,128)S(1)}, f32[256,128]{0,1:T(8,128)S(1)}, u32[]{:S(2)}, u32[]{:S(2)}) collective-permute-start(f32[256,128]{0,1:T(8,128)S(1)} %fusion.7), channel_id=1, source_target_pairs={{0,256},{128,384},{256,0},{384,128},{1,257},{129,385},{257,1},{385... | collective-permute-start | bytes 393224 | tf_op jit(solution)/shard_map/ppermute | solution.py:191
  80.0 3.6 %collective-permute-done.1 = f32[256,128]{0,1:T(8,128)S(1)} collective-permute-done((f32[256,128]{0,1:T(8,128)S(1)}, f32[256,128]{0,1:T(8,128)S(1)}, u32[]{:S(2)}, u32[]{:S(2)}) %collective-permute-start.1) | collective-permute-done | bytes 131104 | tf_op jit(solution)/shard_map/ppermute | solution.py:191
  83.6 0.7 copy.23
  84.3 0.7 copy.22
  (15 shorter events, 0.1 us)
Async XLA Ops:
  0.6 1.0 %copy-start.5 = (f32[128,128]{1,0:T(8,128)S(1)}, f32[128,128]{1,0:T(8,128)}, u32[]{:S(2)}) copy-start(f32[128,128]{1,0:T(8,128)} %param.12) | copy-start | bytes 196612
  1.6 0.8 copy-start.6
  3.4 38.2 %all-to-all-start = ((f32[128,1,384]{2,1,0:T(1,128)}), f32[128,1,384]{2,1,0:T(1,128)S(1)}, u32[]{:S(2)}, u32[]{:S(2)}) async-start(f32[128,1,384]{2,1,0:T(1,128)} %reshape.171), calls=%async_computation | async-start | bytes 393216 | tf_op jit(solution)/shard_map/all_to_all | solution.py:182
  27.1 14.5 %copy-start.3 = (bf16[256,256]{1,0:T(8,128)(2,1)S(1)}, bf16[256,256]{1,0:T(8,128)(2,1)}, u32[]{:S(2)}) copy-start(bf16[256,256]{1,0:T(8,128)(2,1)} %constant.42.clone.low_ref) | copy-start | bytes 393220
  27.1 14.5 %copy-start.4 = (bf16[256,256]{1,0:T(8,128)(2,1)S(1)}, bf16[256,256]{1,0:T(8,128)(2,1)}, u32[]{:S(2)}) copy-start(bf16[256,256]{1,0:T(8,128)(2,1)} %constant.41.clone.high_ref) | copy-start | bytes 393220
  27.1 14.5 %copy-start = (f32[2,128,128]{2,1,0:T(8,128)S(1)}, f32[2,128,128]{2,1,0:T(8,128)}, u32[]{:S(2)}) copy-start(f32[2,128,128]{2,1,0:T(8,128)} %constant.45.clone.twiddle_ref) | copy-start | bytes 393220
  27.1 14.5 %copy-start.1 = (bf16[256,256]{1,0:T(8,128)(2,1)S(1)}, bf16[256,256]{1,0:T(8,128)(2,1)}, u32[]{:S(2)}) copy-start(bf16[256,256]{1,0:T(8,128)(2,1)} %constant.44.clone.low_t_ref) | copy-start | bytes 393220
  27.2 14.5 %copy-start.2 = (bf16[256,256]{1,0:T(8,128)(2,1)S(1)}, bf16[256,256]{1,0:T(8,128)(2,1)}, u32[]{:S(2)}) copy-start(bf16[256,256]{1,0:T(8,128)(2,1)} %constant.43.clone.high_t_ref) | copy-start | bytes 393220
  69.0 6.5 %collective-permute-start = (f32[256,128]{0,1:T(8,128)S(1)}, f32[256,128]{0,1:T(8,128)S(1)}, u32[]{:S(2)}, u32[]{:S(2)}) collective-permute-start(f32[256,128]{0,1:T(8,128)S(1)} %bitcast.23), channel_id=1, source_target_pairs={{0,128},{128,0},{256,384},{384,256},{1,129},{129,1},{257,385},{385... | collective-permute-start | bytes 393224 | tf_op jit(solution)/shard_map/ppermute | solution.py:191
  75.5 8.1 %collective-permute-start.1 = (f32[256,128]{0,1:T(8,128)S(1)}, f32[256,128]{0,1:T(8,128)S(1)}, u32[]{:S(2)}, u32[]{:S(2)}) collective-permute-start(f32[256,128]{0,1:T(8,128)S(1)} %fusion.7), channel_id=1, source_target_pairs={{0,256},{128,384},{256,0},{384,128},{1,257},{129,385},{257,1},{385... | collective-permute-start | bytes 393224 | tf_op jit(solution)/shard_map/ppermute | solution.py:191

commit v2 on v1

--- a/solution.py
+++ b/solution.py
@@ -129,14 +129,14 @@
     block_t = (high_t_ref[...], low_t_ref[...])
     twiddle = (twiddle_ref[0], twiddle_ref[1])
     kernel = (phase_ref[0], phase_ref[1])
-    sampled = (sample(field_ref[:, :size]), sample(field_ref[:, size : 2 * size]))
-    wave = propagate(sampled, block, block_t, twiddle, kernel, size)
+    object_re, object_im, measured = (field_ref[pl.ds(part, size, stride=3), :] for part in range(3))
+    wave = propagate((sample(object_re), sample(object_im)), block, block_t, twiddle, kernel, size)
     power = wave[0] * wave[0] + wave[1] * wave[1]
-    kept = 1.0 - jnp.sqrt(field_ref[:, 2 * size :] / jnp.maximum(power, 0.01))
+    kept = 1.0 - jnp.sqrt(measured / jnp.maximum(power, 0.01))
     residual = (kept * wave[0], kept * wave[1])
     back = propagate(residual, block, block_t, twiddle, conj(kernel), size)
-    out_ref[:, :size] = spread(back[0])
-    out_ref[:, size:] = spread(back[1])
+    for part in range(2):
+        out_ref[pl.ds(part, size, stride=2), :] = spread(back[part])
 
 
 def fresnel_phase(fresnel_now, size):
@@ -155,7 +155,7 @@
     vmem = pl.BlockSpec(memory_space=pltpu.VMEM)
     return pl.pallas_call(
         partial(column_kernel, size),
-        out_shape=jax.ShapeDtypeStruct((size, 2 * size), F32),
+        out_shape=jax.ShapeDtypeStruct((2 * size, size), F32),
         in_specs=[pl.BlockSpec(memory_space=pltpu.SMEM)] + [vmem] * 7,
         out_specs=vmem,
         compiler_params=pltpu.CompilerParams(vmem_limit_bytes=32 * 1024 * 1024),
@@ -173,23 +173,48 @@
     )
 
 
+def pack_kernel(size, re_ref, im_ref, intensity_ref, out_ref):
+    for part, ref in enumerate((re_ref, im_ref, intensity_ref)):
+        out_ref[pl.ds(part, size, stride=3), :] = ref[...].T
+
+
+def finish_kernel(size, count, tiles_ref, re_ref, im_ref):
+    for part, ref in enumerate((re_ref, im_ref)):
+        total = tiles_ref[pl.ds(part, size, stride=2), :]
+        for other in range(1, count):
+            total = total + tiles_ref[pl.ds(2 * size * other + part, size, stride=2), :]
+        ref[...] = total.T
+
+
+def exchange(rows):
+    moved = lax.all_to_all(rows[:, None, :], "tile", split_axis=0, concat_axis=0, tiled=True)
+    return moved[:, 0, :]
+
+
 def body(object_re, object_im, intensity, shrink, offset, fresnel):
     size = object_re.shape[0]
-    tile_count = lax.axis_size("tile")
+    dist_count = lax.axis_size("dist")
+    vmem = pl.BlockSpec(memory_space=pltpu.VMEM)
     phase = fresnel_phase(fresnel[0], size)
-    columns = jnp.concatenate([object_re.T, object_im.T, intensity[0].T], axis=1)
-    columns = columns.reshape(tile_count, 1, 3 * size)
-    field = lax.all_to_all(columns, "tile", split_axis=0, concat_axis=0, tiled=True)
-    field = field.reshape(tile_count, 3 * size)
+    columns = pl.pallas_call(
+        partial(pack_kernel, size),
+        out_shape=jax.ShapeDtypeStruct((3 * size, size), F32),
+        in_specs=[vmem] * 3,
+        out_specs=vmem,
+        name="pack",
+    )(object_re, object_im, intensity[0])
+    field = exchange(columns)
     gradient = run_column(jnp.concatenate([shrink, offset]), field, phase, size)
-    tiles = lax.all_to_all(
-        gradient.reshape(tile_count, 1, 2 * size), "tile", split_axis=0, concat_axis=0, tiled=True
-    ).reshape(tile_count, 2 * size)
-    total = tiles.T
-    for partner in (1, 2):
-        pairs = [(i, i ^ partner) for i in range(lax.axis_size("dist"))]
-        total = total + lax.ppermute(total, "dist", pairs)
-    return (total[:size], total[size:])
+    tiles = exchange(gradient)
+    tiles = lax.all_gather(tiles, "dist", axis=0, tiled=True)
+    out = jax.ShapeDtypeStruct((size, size), F32)
+    return pl.pallas_call(
+        partial(finish_kernel, size, dist_count),
+        out_shape=(out, out),
+        in_specs=[vmem],
+        out_specs=(vmem, vmem),
+        name="finish",
+    )(tiles)
 
 
 def solution(mesh):

time: 85.4 us -> 82.4 us (0.965)
  blocking collectives: 24.1 us -> 36.6 us
  starting transfers between devices: 31.4 us -> 21.5 us
  waiting for transfers between devices: 18.9 us -> 14.4 us
  local copies, waits for them, and re-layouts: 4.35 us -> 0.02 us
  Pallas kernels: 3.05 us -> 6.56 us
    all_gather x0 -> x1, blocking collectives: none -> 12.5 us  [body(): tiles = lax.all_gather(tiles, 'dist', axis=0, tiled=True)]
    ppermute x2 -> x0, starting transfers between devices: 10 us -> none  [body(): total = total + lax.ppermute(total, 'dist', pairs)]
    ppermute x2 -> x0, waiting for transfers between devices: 4.55 us -> none  [body(): total = total + lax.ppermute(total, 'dist', pairs)]
    pallas_call x0 -> x2, Pallas kernels: none -> 3.51 us  [the longest x1 1.8 us: body(): pl.pallas_call(partial(finish_kernel, size, dist_count), out_shape=(out,...]
    unnamed x21 -> x10, local copies, waits for them, and re-layouts: 3.39 us -> 0.02 us
    reshape x2 -> x0, local copies, waits for them, and re-layouts: 0.95 us -> none  [the longest x1 0.81 us: body(): columns = columns.reshape(tile_count, 1, 3 * size)]
  transfers between devices with their start and end apart: 3 -> 1, of which waited for: 3 -> 1; matrix products, arithmetic and copies ran while one was open for 0% -> 0% of each run, Pallas kernels for 0% -> 0%
where the time goes in v2:
time: 82.4 us; the launch traced here: 82.1 us
  blocking collectives  36.6 us (44%)
  starting transfers between devices  21.5 us (26%)
  waiting for transfers between devices  14.4 us (17%)
  Pallas kernels  6.56 us (8%)
  between operations  2.64 us (3%)
    all_to_all x1, blocking collectives, exchange(): lax.all_to_all(rows[:, None, :], 'tile', split_axis=0, concat_axis=0, til...  24.1 us
    all_to_all x1, starting transfers between devices, exchange(): lax.all_to_all(rows[:, None, :], 'tile', split_axis=0, concat_axis=0, til...  21.5 us
    all_to_all x1, waiting for transfers between devices, exchange(): lax.all_to_all(rows[:, None, :], 'tile', split_axis=0, concat_axis=0, til...  14.4 us
    all_gather x1, blocking collectives, body(): tiles = lax.all_gather(tiles, 'dist', axis=0, tiled=True)  12.5 us
    pallas_call x1, Pallas kernels, run_column(): pl.pallas_call(partial(column_kernel, size), out_shape=jax.ShapeDtypeStru...  3.05 us
    pallas_call x1, Pallas kernels, body(): pl.pallas_call(partial(finish_kernel, size, dist_count), out_shape=(out,...  1.8 us
    pallas_call x1, Pallas kernels, body(): pl.pallas_call(partial(pack_kernel, size), out_shape=jax.ShapeDtypeStruct...  1.71 us
  transfers between devices with their start and end apart: 1, of which 1 were waited for; matrix products, arithmetic and copies ran while one was open for 0% of the time, Pallas kernels for 0%

profile of v2, /device:TPU:1, one launch (start us, length us, event | category | flops | bytes accessed | tf_op | source)
XLA Modules:
  0.0 82.1 jit_solution(1386033750854476998)
XLA Ops:
  0.6 1.7 %pack.1 = f32[384,128]{1,0:T(8,128)} custom-call(f32[128,128]{1,0:T(8,128)} %re_ref.1, f32[128,128]{1,0:T(8,128)} %im_ref.1, f32[128,128]{1,0:T(8,128)} %bitcast.17), custom_call_target="tpu_custom_call" | custom-call | tf_op jit(solution)/shard_map/pack/pallas_call | solution.py:199
  2.3 0.0 copy-start.3
  2.3 0.0 copy-start.4
  2.3 21.5 %all-to-all-start = ((f32[384,1,128]{2,1,0:T(1,128)}), f32[384,1,128]{2,1,0:T(1,128)S(1)}, u32[]{:S(2)}, u32[]{:S(2)}) async-start(f32[384,1,128]{2,1,0:T(1,128)} %bitcast.15), calls=%async_computation | async-start | bytes 393216 | tf_op jit(solution)/shard_map/all_to_all | solution.py:190
  25.8 0.1 pad_add_fusion.scalars
  25.9 0.0 copy-start.2
  25.9 0.3 fusion.6
  26.2 0.0 copy-start
  26.2 0.0 copy-start.1
  26.2 14.4 %all-to-all-done = f32[384,1,128]{2,1,0:T(1,128)S(1)} async-done(((f32[384,1,128]{2,1,0:T(1,128)}), f32[384,1,128]{2,1,0:T(1,128)S(1)}, u32[]{:S(2)}, u32[]{:S(2)}) %all-to-all-start) | async-done | bytes 196640 | tf_op jit(solution)/shard_map/all_to_all | solution.py:190
  40.7 0.0 copy-done.3
  40.7 0.0 copy-done.4
  40.7 0.0 copy-done.2
  40.7 0.0 copy-done
  40.7 0.0 copy-done.1
  40.7 3.1 %column.1 = f32[256,128]{1,0:T(8,128)S(1)} custom-call(s32[2]{0:T(128)S(1)} %pad_add_fusion.scalars, f32[384,128]{1,0:T(8,128)S(1)} %bitcast.12, f32[2,128,128]{2,1,0:T(8,128)S(1)} %maximum_multiply_fusion.phase_ref, bf16[256,256]{1,0:T(8,128)(2,1)S(1)} %copy-done.4, bf16[256,256]{1,0:T(8,128)(2,1)S(1)} %copy-done.3, bf16[256,256]{1,0:T(8,128)(2,1)S(1)} %copy-done.2, ...), custom_call_target="tpu_custom_call" | custom-call | tf_op jit(solution)/shard_map/column/pallas_call | solution.py:156
  43.7 24.1 %all_to_all.10 = f32[256,1,128]{2,1,0:T(1,128)S(1)} all-to-all(f32[256,1,128]{2,1,0:T(1,128)S(1)} %bitcast.13), channel_id=1, replica_groups=mesh['dist'=4,'tile'=128] {'tile'}, dimensions={0} | all-to-all | bytes 262144 | tf_op jit(solution)/shard_map/all_to_all | solution.py:190
  67.9 12.5 %all-gather = f32[1024,1,128]{2,0,1:T(8,128)} all-gather(f32[256,1,128]{2,0,1:T(8,128)S(1)} %bitcast.16), channel_id=2, replica_groups=mesh['dist'=4,'tile'=128] {'dist'}, dimensions={0}, use_global_device_ids=true | all-gather | bytes 655360 | tf_op jit(solution)/shard_map/all_gather | solution.py:209
  80.3 1.8 %finish.1 = (f32[128,128]{1,0:T(8,128)}, f32[128,128]{1,0:T(8,128)}) custom-call(f32[1024,128]{1,0:T(8,128)} %bitcast.14), custom_call_target="tpu_custom_call" | custom-call | tf_op jit(solution)/shard_map/finish/pallas_call | solution.py:211
  (2 shorter events, 0.0 us)
Async XLA Ops:
  2.3 38.3 %copy-start.3 = (bf16[256,256]{1,0:T(8,128)(2,1)S(1)}, bf16[256,256]{1,0:T(8,128)(2,1)}, u32[]{:S(2)}) copy-start(bf16[256,256]{1,0:T(8,128)(2,1)} %constant.42.clone.low_ref) | copy-start | bytes 393220
  2.3 38.3 %copy-start.4 = (bf16[256,256]{1,0:T(8,128)(2,1)S(1)}, bf16[256,256]{1,0:T(8,128)(2,1)}, u32[]{:S(2)}) copy-start(bf16[256,256]{1,0:T(8,128)(2,1)} %constant.41.clone.high_ref) | copy-start | bytes 393220
  2.3 38.3 %all-to-all-start = ((f32[384,1,128]{2,1,0:T(1,128)}), f32[384,1,128]{2,1,0:T(1,128)S(1)}, u32[]{:S(2)}, u32[]{:S(2)}) async-start(f32[384,1,128]{2,1,0:T(1,128)} %bitcast.15), calls=%async_computation | async-start | bytes 393216 | tf_op jit(solution)/shard_map/all_to_all | solution.py:190
  25.9 14.8 %copy-start.2 = (bf16[256,256]{1,0:T(8,128)(2,1)S(1)}, bf16[256,256]{1,0:T(8,128)(2,1)}, u32[]{:S(2)}) copy-start(bf16[256,256]{1,0:T(8,128)(2,1)} %constant.43.clone.high_t_ref) | copy-start | bytes 393220
  26.2 14.5 %copy-start = (f32[2,128,128]{2,1,0:T(8,128)S(1)}, f32[2,128,128]{2,1,0:T(8,128)}, u32[]{:S(2)}) copy-start(f32[2,128,128]{2,1,0:T(8,128)} %constant.45.clone.twiddle_ref) | copy-start | bytes 393220
  26.2 14.5 %copy-start.1 = (bf16[256,256]{1,0:T(8,128)(2,1)S(1)}, bf16[256,256]{1,0:T(8,128)(2,1)}, u32[]{:S(2)}) copy-start(bf16[256,256]{1,0:T(8,128)(2,1)} %constant.44.clone.low_t_ref) | copy-start | bytes 393220

commit v3 on v2

--- a/solution.py
+++ b/solution.py
@@ -11,12 +11,20 @@
 
 F32 = jnp.float32
 BF16 = jnp.bfloat16
+LAYERS = 16
 
 
 def two_terms(values):
     high = values.astype(BF16)
     low = (values - high.astype(np.float32)).astype(BF16)
     return high, low
+
+
+def tile_order(size):
+    inner = size // LAYERS
+    bits = LAYERS.bit_length() - 1
+    layers = [int(format(layer, f"0{bits}b")[::-1], 2) for layer in range(LAYERS)]
+    return layers, [place * LAYERS + layer for layer in layers for place in range(inner)]
 
 
 def constant_tables(size):
@@ -24,10 +32,16 @@
     product = np.outer(index, index)
     angle = 2.0 * np.pi / size * (product % size)
     real, imag = np.cos(angle), -np.sin(angle)
-    block = np.block([[real, -imag], [imag, real]]).astype(np.float32)
+    inner = size // LAYERS
+    tile = index % inner * LAYERS + index // inner
+    tables = []
+    for order in (tile, index):
+        part, other = real[:, order], imag[:, order]
+        block = np.block([[part, -other], [other, part]]).astype(np.float32)
+        tables += two_terms(block) + two_terms(block.T)
     angle = 2.0 * np.pi / (size * size) * product
     twiddle = np.stack([np.cos(angle), -np.sin(angle)]).astype(np.float32)
-    return two_terms(block) + (twiddle,)
+    return np.concatenate(tables), twiddle
 
 
 def split(values):
@@ -51,7 +65,9 @@
     return (pair[0], -pair[1])
 
 
-def propagate(values, block, block_t, twiddle, kernel, size):
+def propagate(values, tables, twiddle, kernel, size):
+    rows, rows_t, lanes, lanes_t = tables
+
     def by_rows(table, pair):
         out = product(table, split(jnp.concatenate(pair, axis=0)))
         return (out[:size], out[size:])
@@ -60,15 +76,18 @@
         out = product(split(jnp.concatenate(pair, axis=1)), table)
         return (out[:, :size], out[:, size:])
 
-    mixed = times(by_rows(block, values), twiddle)
-    spectrum = times(by_lanes(mixed, block_t), kernel)
-    mixed = times(by_lanes(spectrum, block), conj(twiddle))
-    return by_rows(block_t, mixed)
-
-
-def column_kernel(size, scalars, field_ref, phase_ref, high_ref, low_ref, high_t_ref, low_t_ref, twiddle_ref, out_ref):
+    mixed = times(by_rows(rows, values), twiddle)
+    spectrum = times(by_lanes(mixed, lanes_t), kernel)
+    mixed = times(by_lanes(spectrum, lanes), conj(twiddle))
+    return by_rows(rows_t, mixed)
+
+
+def column_kernel(size, scalars, field_ref, phase_ref, table_ref, twiddle_ref, out_ref):
     shape = (size, size)
-    row = lax.broadcasted_iota(jnp.int32, shape, 0)
+    inner = size // LAYERS
+    slots = tile_order(size)[0]
+    line = lax.broadcasted_iota(jnp.int32, shape, 0)
+    row = line % inner * LAYERS + line // inner
     lane = lax.broadcasted_iota(jnp.int32, shape, 1)
     total = size * size
     bits = total.bit_length() - 1
@@ -78,19 +97,21 @@
         centre = total // 2
         return centre * total + (index - centre) * (total - shrink) + offset * total
 
-    place = scaled(row * size + lane)
-    weight = jnp.bitwise_and(place, total - 1).astype(F32) * (1.0 / total)
+    position = scaled(row * size + lane)
+    weight = jnp.bitwise_and(position, total - 1).astype(F32) * (1.0 / total)
     shift = lax.shift_right_arithmetic(scaled(row * size), bits) - row * size
-    leading = lax.shift_right_arithmetic(place, bits) - (row * size + lane) == shift
+    leading = lax.shift_right_arithmetic(position, bits) - (row * size + lane) == shift
     rest = 1.0 - weight
 
+    place = lax.broadcasted_iota(jnp.int32, (inner, size), 0)
+
     def rows_up(values):
-        moved = pltpu.roll(values, size - 1, 0)
-        return jnp.where(row == size - 1, 0.0, moved)
+        edge = pltpu.roll(values[:inner], inner - 1, 0)
+        return jnp.concatenate([values[inner:], jnp.where(place == inner - 1, 0.0, edge)], axis=0)
 
     def rows_down(values):
-        moved = pltpu.roll(values, 1, 0)
-        return jnp.where(row == 0, 0.0, moved)
+        edge = pltpu.roll(values[size - inner :], 1, 0)
+        return jnp.concatenate([jnp.where(place == 0, 0.0, edge), values[: size - inner]], axis=0)
 
     def lanes(values, index):
         return jnp.take_along_axis(values, jnp.bitwise_and(index, size - 1), axis=1, mode="promise_in_bounds")
@@ -125,18 +146,25 @@
             stay += jnp.where(jnp.logical_or(to_next, to_last), 0.0, moved)
         return stay + rows_down(down) + rows_up(up)
 
-    block = (high_ref[...], low_ref[...])
-    block_t = (high_t_ref[...], low_t_ref[...])
+    def gathered(part, count):
+        pieces = [field_ref[pl.ds(count * inner * slot + part, inner, stride=count), :] for slot in slots]
+        return jnp.concatenate(pieces, axis=0)
+
+    span = 2 * size
+    terms = [table_ref[pl.ds(span * term, span), :] for term in range(8)]
+    tables = [(terms[2 * term], terms[2 * term + 1]) for term in range(4)]
     twiddle = (twiddle_ref[0], twiddle_ref[1])
     kernel = (phase_ref[0], phase_ref[1])
-    object_re, object_im, measured = (field_ref[pl.ds(part, size, stride=3), :] for part in range(3))
-    wave = propagate((sample(object_re), sample(object_im)), block, block_t, twiddle, kernel, size)
+    object_re, object_im, measured = (gathered(part, 3) for part in range(3))
+    wave = propagate((sample(object_re), sample(object_im)), tables, twiddle, kernel, size)
     power = wave[0] * wave[0] + wave[1] * wave[1]
     kept = 1.0 - jnp.sqrt(measured / jnp.maximum(power, 0.01))
     residual = (kept * wave[0], kept * wave[1])
-    back = propagate(residual, block, block_t, twiddle, conj(kernel), size)
+    back = propagate(residual, tables, twiddle, conj(kernel), size)
     for part in range(2):
-        out_ref[pl.ds(part, size, stride=2), :] = spread(back[part])
+        result = spread(back[part])
+        for layer, slot in enumerate(slots):
+            out_ref[pl.ds(2 * inner * slot + part, inner, stride=2), :] = result[inner * layer : inner * (layer + 1)]
 
 
 def fresnel_phase(fresnel_now, size):
@@ -151,12 +179,12 @@
 
 
 def run_column(scalars, field, phase, size, **options):
-    high, low, twiddle = constant_tables(size)
+    tables, twiddle = constant_tables(size)
     vmem = pl.BlockSpec(memory_space=pltpu.VMEM)
     return pl.pallas_call(
         partial(column_kernel, size),
         out_shape=jax.ShapeDtypeStruct((2 * size, size), F32),
-        in_specs=[pl.BlockSpec(memory_space=pltpu.SMEM)] + [vmem] * 7,
+        in_specs=[pl.BlockSpec(memory_space=pltpu.SMEM)] + [vmem] * 4,
         out_specs=vmem,
         compiler_params=pltpu.CompilerParams(vmem_limit_bytes=32 * 1024 * 1024),
         name="column",
@@ -165,10 +193,7 @@
         scalars,
         field,
         phase,
-        jnp.asarray(high),
-        jnp.asarray(low),
-        jnp.asarray(high.T),
-        jnp.asarray(low.T),
+        jnp.asarray(tables),
         jnp.asarray(twiddle),
     )
 
@@ -187,7 +212,8 @@
 
 
 def exchange(rows):
-    moved = lax.all_to_all(rows[:, None, :], "tile", split_axis=0, concat_axis=0, tiled=True)
+    groups = [tile_order(lax.axis_size("tile"))[1]]
+    moved = lax.all_to_all(rows[:, None, :], "tile", 0, 0, axis_index_groups=groups, tiled=True)
     return moved[:, 0, :]
 
 
@@ -213,6 +239,7 @@
         out_shape=(out, out),
         in_specs=[vmem],
         out_specs=(vmem, vmem),
+        compiler_params=pltpu.CompilerParams(vmem_limit_bytes=8 * 1024 * 1024),
         name="finish",
     )(tiles)
 

time: 82.4 us -> 79 us (0.959)
  blocking collectives: 36.6 us -> 34.7 us
  Pallas kernels: 6.56 us -> 5.6 us
    all_to_all x1, blocking collectives: 24.1 us -> 22.7 us  [exchange(): lax.all_to_all(rows[:, None, :], 'tile', 0, 0, axis_index_groups=groups,...]
    pallas_call x1, Pallas kernels: 1.8 us -> 0.76 us  [body(): pl.pallas_call(partial(finish_kernel, size, dist_count), out_shape=(out,...]
  transfers between devices with their start and end apart: 1 -> 1, of which waited for: 1 -> 1; matrix products, arithmetic and copies ran while one was open for 0% -> 1% of each run, Pallas kernels for 0% -> 0%
where the time goes in v3:
time: 79 us; the launch traced here: 78.7 us
  blocking collectives  34.7 us (44%)
  starting transfers between devices  21.3 us (27%)
  waiting for transfers between devices  14 us (18%)
  Pallas kernels  5.6 us (7%)
  between operations  2.62 us (3%)
    all_to_all x1, blocking collectives, exchange(): lax.all_to_all(rows[:, None, :], 'tile', 0, 0, axis_index_groups=groups,...  22.7 us
    all_to_all x1, starting transfers between devices, exchange(): lax.all_to_all(rows[:, None, :], 'tile', 0, 0, axis_index_groups=groups,...  21.3 us
    all_to_all x1, waiting for transfers between devices, exchange(): lax.all_to_all(rows[:, None, :], 'tile', 0, 0, axis_index_groups=groups,...  14 us
    all_gather x1, blocking collectives, body(): tiles = lax.all_gather(tiles, 'dist', axis=0, tiled=True)  12 us
    pallas_call x1, Pallas kernels, run_column(): pl.pallas_call(partial(column_kernel, size), out_shape=jax.ShapeDtypeStru...  3.05 us
    pallas_call x1, Pallas kernels, body(): pl.pallas_call(partial(pack_kernel, size), out_shape=jax.ShapeDtypeStruct...  1.8 us
  transfers between devices with their start and end apart: 1, of which 1 were waited for; matrix products, arithmetic and copies ran while one was open for 1% of the time, Pallas kernels for 0%

profile of v3, /device:TPU:1, one launch (start us, length us, event | category | flops | bytes accessed | tf_op | source)
XLA Modules:
  0.0 78.7 jit_solution(10872052249559921580)
XLA Ops:
  0.6 0.0 copy-start
  0.6 1.8 %pack.1 = f32[384,128]{1,0:T(8,128)} custom-call(f32[128,128]{1,0:T(8,128)} %re_ref.1, f32[128,128]{1,0:T(8,128)} %im_ref.1, f32[128,128]{1,0:T(8,128)} %bitcast.17), custom_call_target="tpu_custom_call" | custom-call | tf_op jit(solution)/shard_map/pack/pallas_call | solution.py:225
  2.4 21.3 %all-to-all-start = ((f32[384,1,128]{2,1,0:T(1,128)}), f32[384,1,128]{2,1,0:T(1,128)S(1)}, u32[]{:S(2)}, u32[]{:S(2)}) async-start(f32[384,1,128]{2,1,0:T(1,128)} %bitcast.15), calls=%async_computation | async-start | bytes 393216 | tf_op jit(solution)/shard_map/all_to_all | solution.py:216
  25.7 0.1 pad_add_fusion.scalars
  25.8 0.3 fusion.6
  26.1 0.0 copy-start.1
  26.2 14.0 %all-to-all-done = f32[384,1,128]{2,1,0:T(1,128)S(1)} async-done(((f32[384,1,128]{2,1,0:T(1,128)}), f32[384,1,128]{2,1,0:T(1,128)S(1)}, u32[]{:S(2)}, u32[]{:S(2)}) %all-to-all-start) | async-done | bytes 196640 | tf_op jit(solution)/shard_map/all_to_all | solution.py:216
  40.2 0.0 copy-done
  40.2 0.0 copy-done.1
  40.2 3.0 %column.1 = f32[256,128]{1,0:T(8,128)S(1)} custom-call(s32[2]{0:T(128)S(1)} %pad_add_fusion.scalars, f32[384,128]{1,0:T(8,128)S(1)} %bitcast.13, f32[2,128,128]{2,1,0:T(8,128)S(1)} %maximum_multiply_fusion.phase_ref, bf16[2048,256]{1,0:T(8,128)(2,1)S(1)} %copy-done, f32[2,128,128]{2,1,0:T(8,128)S(1)} %copy-done.1), custom_call_target="tpu_custom_call" | custom-call | tf_op jit(solution)/shard_map/column/pallas_call | solution.py:184
  43.2 22.7 %all_to_all.10 = f32[256,1,128]{2,1,0:T(1,128)S(1)} all-to-all(f32[256,1,128]{2,1,0:T(1,128)S(1)} %bitcast.14), channel_id=1, replica_groups={{0,16,32,48,64,80,96,112,8,24,40,56,72,88,104,120,4,20,36,52,68,84,100,..., dimensions={0} | all-to-all | bytes 262144 | tf_op jit(solution)/shard_map/all_to_all | solution.py:216
  65.9 12.0 %all-gather = f32[1024,1,128]{2,0,1:T(8,128)S(1)} all-gather(f32[256,1,128]{2,0,1:T(8,128)S(1)} %bitcast.16), channel_id=2, replica_groups=mesh['dist'=4,'tile'=128] {'dist'}, dimensions={0}, use_global_device_ids=true | all-gather | bytes 655360 | tf_op jit(solution)/shard_map/all_gather | solution.py:235
  78.0 0.8 finish.1
  (2 shorter events, 0.0 us)
Async XLA Ops:
  0.6 39.6 %copy-start = (bf16[2048,256]{1,0:T(8,128)(2,1)S(1)}, bf16[2048,256]{1,0:T(8,128)(2,1)}, u32[]{:S(2)}) copy-start(bf16[2048,256]{1,0:T(8,128)(2,1)} %constant.35.clone.table_ref) | copy-start | bytes 3145732
  2.4 37.7 %all-to-all-start = ((f32[384,1,128]{2,1,0:T(1,128)}), f32[384,1,128]{2,1,0:T(1,128)S(1)}, u32[]{:S(2)}, u32[]{:S(2)}) async-start(f32[384,1,128]{2,1,0:T(1,128)} %bitcast.15), calls=%async_computation | async-start | bytes 393216 | tf_op jit(solution)/shard_map/all_to_all | solution.py:216
  26.1 14.0 %copy-start.1 = (f32[2,128,128]{2,1,0:T(8,128)S(1)}, f32[2,128,128]{2,1,0:T(8,128)}, u32[]{:S(2)}) copy-start(f32[2,128,128]{2,1,0:T(8,128)} %constant.36.clone.twiddle_ref) | copy-start | bytes 393220

commit v4 on v3

--- a/solution.py
+++ b/solution.py
@@ -20,11 +20,19 @@
     return high, low
 
 
+def place_of(index, inner):
+    return (index + 3 * inner // 4) % inner
+
+
+def layer_slots():
+    bits = LAYERS.bit_length() - 1
+    return [int(format(layer ^ LAYERS // 2, f"0{bits}b")[::-1], 2) for layer in range(LAYERS)]
+
+
 def tile_order(size):
     inner = size // LAYERS
-    bits = LAYERS.bit_length() - 1
-    layers = [int(format(layer, f"0{bits}b")[::-1], 2) for layer in range(LAYERS)]
-    return layers, [place * LAYERS + layer for layer in layers for place in range(inner)]
+    layers = sorted(range(LAYERS), key=layer_slots().__getitem__)
+    return [place_of(index, inner) * LAYERS + layer for layer in layers for index in range(inner)]
 
 
 def constant_tables(size):
@@ -33,7 +41,7 @@
     angle = 2.0 * np.pi / size * (product % size)
     real, imag = np.cos(angle), -np.sin(angle)
     inner = size // LAYERS
-    tile = index % inner * LAYERS + index // inner
+    tile = place_of(index % inner, inner) * LAYERS + index // inner
     tables = []
     for order in (tile, index):
         part, other = real[:, order], imag[:, order]
@@ -85,9 +93,9 @@
 def column_kernel(size, scalars, field_ref, phase_ref, table_ref, twiddle_ref, out_ref):
     shape = (size, size)
     inner = size // LAYERS
-    slots = tile_order(size)[0]
+    slots = layer_slots()
     line = lax.broadcasted_iota(jnp.int32, shape, 0)
-    row = line % inner * LAYERS + line // inner
+    row = place_of(line % inner, inner) * LAYERS + line // inner
     lane = lax.broadcasted_iota(jnp.int32, shape, 1)
     total = size * size
     bits = total.bit_length() - 1
@@ -103,7 +111,7 @@
     leading = lax.shift_right_arithmetic(position, bits) - (row * size + lane) == shift
     rest = 1.0 - weight
 
-    place = lax.broadcasted_iota(jnp.int32, (inner, size), 0)
+    place = place_of(lax.broadcasted_iota(jnp.int32, (inner, size), 0), inner)
 
     def rows_up(values):
         edge = pltpu.roll(values[:inner], inner - 1, 0)
@@ -212,7 +220,7 @@
 
 
 def exchange(rows):
-    groups = [tile_order(lax.axis_size("tile"))[1]]
+    groups = [tile_order(lax.axis_size("tile"))]
     moved = lax.all_to_all(rows[:, None, :], "tile", 0, 0, axis_index_groups=groups, tiled=True)
     return moved[:, 0, :]
 

time: 79 us -> 71.7 us (0.908)
  waiting for transfers between devices: 14 us -> 6.35 us
  starting transfers between devices: 21.3 us -> 24.6 us
  blocking collectives: 34.7 us -> 31.9 us
    all_to_all x1, waiting for transfers between devices: 14 us -> 6.35 us  [exchange(): lax.all_to_all(rows[:, None, :], 'tile', 0, 0, axis_index_groups=groups,...]
    all_to_all x1, starting transfers between devices: 21.3 us -> 24.6 us  [exchange(): lax.all_to_all(rows[:, None, :], 'tile', 0, 0, axis_index_groups=groups,...]
    all_gather x1, blocking collectives: 12 us -> 10.4 us  [body(): tiles = lax.all_gather(tiles, 'dist', axis=0, tiled=True)]
    all_to_all x1, blocking collectives: 22.7 us -> 21.5 us  [exchange(): lax.all_to_all(rows[:, None, :], 'tile', 0, 0, axis_index_groups=groups,...]
where the time goes in v4:
time: 71.7 us; the launch traced here: 71.4 us
  blocking collectives  31.9 us (44%)
  starting transfers between devices  24.6 us (34%)
  waiting for transfers between devices  6.35 us (9%)
  Pallas kernels  5.6 us (8%)
  between operations  2.62 us (4%)
    all_to_all x1, starting transfers between devices, exchange(): lax.all_to_all(rows[:, None, :], 'tile', 0, 0, axis_index_groups=groups,...  24.6 us
    all_to_all x1, blocking collectives, exchange(): lax.all_to_all(rows[:, None, :], 'tile', 0, 0, axis_index_groups=groups,...  21.5 us
    all_gather x1, blocking collectives, body(): tiles = lax.all_gather(tiles, 'dist', axis=0, tiled=True)  10.4 us
    all_to_all x1, waiting for transfers between devices, exchange(): lax.all_to_all(rows[:, None, :], 'tile', 0, 0, axis_index_groups=groups,...  6.35 us
    pallas_call x1, Pallas kernels, run_column(): pl.pallas_call(partial(column_kernel, size), out_shape=jax.ShapeDtypeStru...  3.05 us
    pallas_call x1, Pallas kernels, body(): pl.pallas_call(partial(pack_kernel, size), out_shape=jax.ShapeDtypeStruct...  1.8 us
  transfers between devices with their start and end apart: 1, of which 1 were waited for; matrix products, arithmetic and copies ran while one was open for 1% of the time, Pallas kernels for 0%

profile of v4, /device:TPU:1, one launch (start us, length us, event | category | flops | bytes accessed | tf_op | source)
XLA Modules:
  0.0 71.4 jit_solution(5090434275867259889)
XLA Ops:
  0.6 0.0 copy-start
  0.6 1.8 %pack.1 = f32[384,128]{1,0:T(8,128)} custom-call(f32[128,128]{1,0:T(8,128)} %re_ref.1, f32[128,128]{1,0:T(8,128)} %im_ref.1, f32[128,128]{1,0:T(8,128)} %bitcast.17), custom_call_target="tpu_custom_call" | custom-call | tf_op jit(solution)/shard_map/pack/pallas_call | solution.py:233
  2.4 24.6 %all-to-all-start = ((f32[384,1,128]{2,1,0:T(1,128)}), f32[384,1,128]{2,1,0:T(1,128)S(1)}, u32[]{:S(2)}, u32[]{:S(2)}) async-start(f32[384,1,128]{2,1,0:T(1,128)} %bitcast.15), calls=%async_computation | async-start | bytes 393216 | tf_op jit(solution)/shard_map/all_to_all | solution.py:224
  29.0 0.1 pad_add_fusion.scalars
  29.0 0.3 fusion.6
  29.4 0.0 copy-start.1
  29.4 6.3 %all-to-all-done = f32[384,1,128]{2,1,0:T(1,128)S(1)} async-done(((f32[384,1,128]{2,1,0:T(1,128)}), f32[384,1,128]{2,1,0:T(1,128)S(1)}, u32[]{:S(2)}, u32[]{:S(2)}) %all-to-all-start) | async-done | bytes 196640 | tf_op jit(solution)/shard_map/all_to_all | solution.py:224
  35.7 0.0 copy-done
  35.7 0.0 copy-done.1
  35.7 3.0 %column.1 = f32[256,128]{1,0:T(8,128)S(1)} custom-call(s32[2]{0:T(128)S(1)} %pad_add_fusion.scalars, f32[384,128]{1,0:T(8,128)S(1)} %bitcast.13, f32[2,128,128]{2,1,0:T(8,128)S(1)} %maximum_multiply_fusion.phase_ref, bf16[2048,256]{1,0:T(8,128)(2,1)S(1)} %copy-done, f32[2,128,128]{2,1,0:T(8,128)S(1)} %copy-done.1), custom_call_target="tpu_custom_call" | custom-call | tf_op jit(solution)/shard_map/column/pallas_call | solution.py:192
  38.8 21.5 %all_to_all.10 = f32[256,1,128]{2,1,0:T(1,128)S(1)} all-to-all(f32[256,1,128]{2,1,0:T(1,128)S(1)} %bitcast.14), channel_id=1, replica_groups={{104,120,8,24,40,56,72,88,96,112,0,16,32,48,64,80,108,124,12,28,44,60,7..., dimensions={0} | all-to-all | bytes 262144 | tf_op jit(solution)/shard_map/all_to_all | solution.py:224
  60.3 10.4 %all-gather = f32[1024,1,128]{2,0,1:T(8,128)S(1)} all-gather(f32[256,1,128]{2,0,1:T(8,128)S(1)} %bitcast.16), channel_id=2, replica_groups=mesh['dist'=4,'tile'=128] {'dist'}, dimensions={0}, use_global_device_ids=true | all-gather | bytes 655360 | tf_op jit(solution)/shard_map/all_gather | solution.py:243
  70.7 0.8 %finish.1 = (f32[128,128]{1,0:T(8,128)}, f32[128,128]{1,0:T(8,128)}) custom-call(f32[1024,128]{1,0:T(8,128)S(1)} %bitcast.12), custom_call_target="tpu_custom_call" | custom-call | tf_op jit(solution)/shard_map/finish/pallas_call | solution.py:245
  (2 shorter events, 0.0 us)
Async XLA Ops:
  0.6 35.1 %copy-start = (bf16[2048,256]{1,0:T(8,128)(2,1)S(1)}, bf16[2048,256]{1,0:T(8,128)(2,1)}, u32[]{:S(2)}) copy-start(bf16[2048,256]{1,0:T(8,128)(2,1)} %constant.35.clone.table_ref) | copy-start | bytes 3145732
  2.4 33.3 %all-to-all-start = ((f32[384,1,128]{2,1,0:T(1,128)}), f32[384,1,128]{2,1,0:T(1,128)S(1)}, u32[]{:S(2)}, u32[]{:S(2)}) async-start(f32[384,1,128]{2,1,0:T(1,128)} %bitcast.15), calls=%async_computation | async-start | bytes 393216 | tf_op jit(solution)/shard_map/all_to_all | solution.py:224
  29.4 6.4 %copy-start.1 = (f32[2,128,128]{2,1,0:T(8,128)S(1)}, f32[2,128,128]{2,1,0:T(8,128)}, u32[]{:S(2)}) copy-start(f32[2,128,128]{2,1,0:T(8,128)} %constant.36.clone.twiddle_ref) | copy-start | bytes 393220

commit v5 on v4

--- a/solution.py
+++ b/solution.py
@@ -154,8 +154,8 @@
             stay += jnp.where(jnp.logical_or(to_next, to_last), 0.0, moved)
         return stay + rows_down(down) + rows_up(up)
 
-    def gathered(part, count):
-        pieces = [field_ref[pl.ds(count * inner * slot + part, inner, stride=count), :] for slot in slots]
+    def gathered(start):
+        pieces = [field_ref[pl.ds(start + 2 * inner * slot, inner, stride=2), :] for slot in slots]
         return jnp.concatenate(pieces, axis=0)
 
     span = 2 * size
@@ -163,8 +163,8 @@
     tables = [(terms[2 * term], terms[2 * term + 1]) for term in range(4)]
     twiddle = (twiddle_ref[0], twiddle_ref[1])
     kernel = (phase_ref[0], phase_ref[1])
-    object_re, object_im, measured = (gathered(part, 3) for part in range(3))
-    wave = propagate((sample(object_re), sample(object_im)), tables, twiddle, kernel, size)
+    measured = jnp.where(core_index() == 0, gathered(1), gathered(span + 1))
+    wave = propagate((sample(gathered(0)), sample(gathered(span))), tables, twiddle, kernel, size)
     power = wave[0] * wave[0] + wave[1] * wave[1]
     kept = 1.0 - jnp.sqrt(measured / jnp.maximum(power, 0.01))
     residual = (kept * wave[0], kept * wave[1])
@@ -172,7 +172,8 @@
     for part in range(2):
         result = spread(back[part])
         for layer, slot in enumerate(slots):
-            out_ref[pl.ds(2 * inner * slot + part, inner, stride=2), :] = result[inner * layer : inner * (layer + 1)]
+            start = size * part + inner * slot
+            out_ref[start : start + inner, :] = result[inner * layer : inner * (layer + 1)]
 
 
 def fresnel_phase(fresnel_now, size):
@@ -194,7 +195,7 @@
         out_shape=jax.ShapeDtypeStruct((2 * size, size), F32),
         in_specs=[pl.BlockSpec(memory_space=pltpu.SMEM)] + [vmem] * 4,
         out_specs=vmem,
-        compiler_params=pltpu.CompilerParams(vmem_limit_bytes=32 * 1024 * 1024),
+        compiler_params=pltpu.CompilerParams(vmem_limit_bytes=16 * 1024 * 1024),
         name="column",
         **options,
     )(
@@ -206,17 +207,25 @@
     )
 
 
-def pack_kernel(size, re_ref, im_ref, intensity_ref, out_ref):
-    for part, ref in enumerate((re_ref, im_ref, intensity_ref)):
-        out_ref[pl.ds(part, size, stride=3), :] = ref[...].T
-
-
-def finish_kernel(size, count, tiles_ref, re_ref, im_ref):
+def core_index():
+    return jnp.bitwise_and(lax.axis_index("dist"), 1)
+
+
+def pack_kernel(size, re_ref, im_ref, intensity_ref, out_ref, tiles, arrived):
+    copies = [pltpu.make_async_copy(intensity_ref, tiles.at[1], arrived.at[1])]
+    for core, ref in enumerate((re_ref, im_ref)):
+        copies.append(pltpu.make_async_copy(ref, tiles.at[0], arrived.at[0]))
+        pl.when(core_index() == core)(copies[-1].start)
+    copies[0].start()
+    copies[1].wait()
+    out_ref[pl.ds(0, size, stride=2), :] = tiles[0].T
+    copies[0].wait()
+    out_ref[pl.ds(1, size, stride=2), :] = tiles[1].T
+
+
+def finish_kernel(size, tiles_ref, re_ref, im_ref):
     for part, ref in enumerate((re_ref, im_ref)):
-        total = tiles_ref[pl.ds(part, size, stride=2), :]
-        for other in range(1, count):
-            total = total + tiles_ref[pl.ds(2 * size * other + part, size, stride=2), :]
-        ref[...] = total.T
+        ref[...] = (tiles_ref[pl.ds(size * part, size), :] + tiles_ref[pl.ds(size * (part + 2), size), :]).T
 
 
 def exchange(rows):
@@ -225,25 +234,30 @@
     return moved[:, 0, :]
 
 
+def of_both_cores(rows):
+    return lax.all_gather(rows, "dist", axis=0, tiled=True, axis_index_groups=[[0, 1], [2, 3]])
+
+
 def body(object_re, object_im, intensity, shrink, offset, fresnel):
     size = object_re.shape[0]
-    dist_count = lax.axis_size("dist")
     vmem = pl.BlockSpec(memory_space=pltpu.VMEM)
     phase = fresnel_phase(fresnel[0], size)
     columns = pl.pallas_call(
         partial(pack_kernel, size),
-        out_shape=jax.ShapeDtypeStruct((3 * size, size), F32),
-        in_specs=[vmem] * 3,
+        out_shape=jax.ShapeDtypeStruct((2 * size, size), F32),
+        in_specs=[pl.BlockSpec(memory_space=pl.ANY)] * 3,
         out_specs=vmem,
+        scratch_shapes=[pltpu.VMEM((2, size, size), F32), pltpu.SemaphoreType.DMA((2,))],
         name="pack",
     )(object_re, object_im, intensity[0])
-    field = exchange(columns)
+    field = of_both_cores(exchange(columns))
     gradient = run_column(jnp.concatenate([shrink, offset]), field, phase, size)
-    tiles = exchange(gradient)
-    tiles = lax.all_gather(tiles, "dist", axis=0, tiled=True)
+    first, second = of_both_cores(gradient).reshape(2, 2, size, size)
+    own = jnp.where(core_index() == 0, first[0] + second[0], first[1] + second[1])
+    tiles = lax.all_gather(exchange(own), "dist", axis=0, tiled=True)
     out = jax.ShapeDtypeStruct((size, size), F32)
     return pl.pallas_call(
-        partial(finish_kernel, size, dist_count),
+        partial(finish_kernel, size),
         out_shape=(out, out),
         in_specs=[vmem],
         out_specs=(vmem, vmem),

time: 71.7 us -> 69.9 us (0.975)
  waiting for transfers between devices: 6.35 us -> 3.19 us
  blocking collectives: 31.9 us -> 33.2 us
    all_to_all x1, waiting for transfers between devices: 6.35 us -> 3.19 us  [exchange(): lax.all_to_all(rows[:, None, :], 'tile', 0, 0, axis_index_groups=groups,...]
    all_gather x1 -> x3, blocking collectives: 10.4 us -> 13.1 us  [the longest x1 8.06 us: body(): tiles = lax.all_gather(exchange(own), 'dist', axis=0, tiled=True)]
    all_to_all x1, blocking collectives: 21.5 us -> 20.1 us  [exchange(): lax.all_to_all(rows[:, None, :], 'tile', 0, 0, axis_index_groups=groups,...]
where the time goes in v5:
time: 69.9 us; the launch traced here: 69.7 us
  blocking collectives  33.2 us (47%)
  starting transfers between devices  24.6 us (35%)
  Pallas kernels  5.6 us (8%)
  waiting for transfers between devices  3.19 us (5%)
  between operations  2.63 us (4%)
    all_to_all x1, starting transfers between devices, exchange(): lax.all_to_all(rows[:, None, :], 'tile', 0, 0, axis_index_groups=groups,...  24.6 us
    all_to_all x1, blocking collectives, exchange(): lax.all_to_all(rows[:, None, :], 'tile', 0, 0, axis_index_groups=groups,...  20.1 us
    all_gather x1, blocking collectives, body(): tiles = lax.all_gather(exchange(own), 'dist', axis=0, tiled=True)  8.06 us
    all_gather x2, blocking collectives, of_both_cores(): lax.all_gather(rows, 'dist', axis=0, tiled=True, axis_index_groups=[[0, 1...  5.06 us
    all_to_all x1, waiting for transfers between devices, exchange(): lax.all_to_all(rows[:, None, :], 'tile', 0, 0, axis_index_groups=groups,...  3.19 us
    pallas_call x1, Pallas kernels, run_column(): pl.pallas_call(partial(column_kernel, size), out_shape=jax.ShapeDtypeStru...  3.05 us
    pallas_call x1, Pallas kernels, body(): pl.pallas_call(partial(pack_kernel, size), out_shape=jax.ShapeDtypeStruct...  1.8 us
  transfers between devices with their start and end apart: 1, of which 1 were waited for; matrix products, arithmetic and copies ran while one was open for 1% of the time, Pallas kernels for 0%

profile of v5, /device:TPU:1, one launch (start us, length us, event | category | flops | bytes accessed | tf_op | source)
XLA Modules:
  0.0 69.7 jit_solution(9182161929202791168)
XLA Ops:
  0.6 0.0 copy-start
  0.6 1.8 %pack.1 = f32[256,128]{1,0:T(8,128)} custom-call(f32[128,128]{1,0:T(8,128)} %re_ref.1, f32[128,128]{1,0:T(8,128)} %im_ref.1, f32[128,128]{1,0:T(8,128)} %bitcast.19), custom_call_target="tpu_custom_call" | custom-call | tf_op jit(solution)/shard_map/pack/pallas_call | solution.py:245
  2.5 24.6 %all-to-all-start = ((f32[256,1,128]{2,1,0:T(1,128)}), f32[256,1,128]{2,1,0:T(1,128)S(1)}, u32[]{:S(2)}, u32[]{:S(2)}) async-start(f32[256,1,128]{2,1,0:T(1,128)} %bitcast.16), calls=%async_computation | async-start | bytes 262144 | tf_op jit(solution)/shard_map/all_to_all | solution.py:233
  29.0 0.1 pad_add_fusion.scalars
  29.1 0.3 fusion.7
  29.4 3.2 %all-to-all-done = f32[256,1,128]{2,1,0:T(1,128)S(1)} async-done(((f32[256,1,128]{2,1,0:T(1,128)}), f32[256,1,128]{2,1,0:T(1,128)S(1)}, u32[]{:S(2)}, u32[]{:S(2)}) %all-to-all-start) | async-done | bytes 131104 | tf_op jit(solution)/shard_map/all_to_all | solution.py:233
  32.6 0.0 copy-start.1
  32.6 3.1 %all-gather = f32[512,1,128]{2,0,1:T(8,128)S(1)} all-gather(f32[256,1,128]{2,0,1:T(8,128)S(1)} %bitcast.15), channel_id=2, replica_groups={{0,128},{256,384},{1,129},{257,385},{2,130},{258,386},{3,131},{259,387}..., dimensions={0}, use_global_device_ids=true | all-gather | bytes 393216 | tf_op jit(solution)/shard_map/all_gather | solution.py:238
  35.7 0.0 copy-done
  35.7 0.0 copy-done.1
  35.7 3.0 %column.1 = f32[256,128]{1,0:T(8,128)S(1)} custom-call(s32[2]{0:T(128)S(1)} %pad_add_fusion.scalars, f32[512,128]{1,0:T(8,128)S(1)} %bitcast.13, f32[2,128,128]{2,1,0:T(8,128)S(1)} %maximum_multiply_fusion.phase_ref, bf16[2048,256]{1,0:T(8,128)(2,1)S(1)} %copy-done, f32[2,128,128]{2,1,0:T(8,128)S(1)} %copy-done.1), custom_call_target="tpu_custom_call" | custom-call | tf_op jit(solution)/shard_map/column/pallas_call | solution.py:193
  38.7 2.0 %all_gather.10 = f32[512,128]{1,0:T(8,128)S(1)} all-gather(f32[256,128]{1,0:T(8,128)S(1)} %column.1), channel_id=1, replica_groups={{0,128},{256,384},{1,129},{257,385},{2,130},{258,386},{3,131},{259,387}..., dimensions={0}, use_global_device_ids=true | all-gather | bytes 393216 | tf_op jit(solution)/shard_map/all_gather | solution.py:238
  40.7 20.1 %all_to_all.10 = f32[128,1,128]{2,1,0:T(1,128)S(1)} all-to-all(f32[128,1,128]{2,1,0:T(1,128)S(1)} %bitcast.17), channel_id=1, replica_groups={{104,120,8,24,40,56,72,88,96,112,0,16,32,48,64,80,108,124,12,28,44,60,7..., dimensions={0} | all-to-all | bytes 131072 | tf_op jit(solution)/shard_map/all_to_all | solution.py:233
  60.8 8.1 %all-gather.1 = f32[512,1,128]{2,0,1:T(8,128)S(1)} all-gather(f32[128,1,128]{2,0,1:T(8,128)S(1)} %bitcast.18), channel_id=3, replica_groups=mesh['dist'=4,'tile'=128] {'dist'}, dimensions={0}, use_global_device_ids=true | all-gather | bytes 327680 | tf_op jit(solution)/shard_map/all_gather | solution.py:257
  68.9 0.8 %finish.1 = (f32[128,128]{1,0:T(8,128)}, f32[128,128]{1,0:T(8,128)}) custom-call(f32[512,128]{1,0:T(8,128)S(1)} %bitcast.14), custom_call_target="tpu_custom_call" | custom-call | tf_op jit(solution)/shard_map/finish/pallas_call | solution.py:259
  (3 shorter events, 0.0 us)
Async XLA Ops:
  0.6 35.0 %copy-start = (bf16[2048,256]{1,0:T(8,128)(2,1)S(1)}, bf16[2048,256]{1,0:T(8,128)(2,1)}, u32[]{:S(2)}) copy-start(bf16[2048,256]{1,0:T(8,128)(2,1)} %constant.44.clone.table_ref) | copy-start | bytes 3145732
  2.5 30.1 %all-to-all-start = ((f32[256,1,128]{2,1,0:T(1,128)}), f32[256,1,128]{2,1,0:T(1,128)S(1)}, u32[]{:S(2)}, u32[]{:S(2)}) async-start(f32[256,1,128]{2,1,0:T(1,128)} %bitcast.16), calls=%async_computation | async-start | bytes 262144 | tf_op jit(solution)/shard_map/all_to_all | solution.py:233
  32.6 3.1 %copy-start.1 = (f32[2,128,128]{2,1,0:T(8,128)S(1)}, f32[2,128,128]{2,1,0:T(8,128)}, u32[]{:S(2)}) copy-start(f32[2,128,128]{2,1,0:T(8,128)} %constant.45.clone.twiddle_ref) | copy-start | bytes 393220

commit v6 on v5

--- a/solution.py
+++ b/solution.py
@@ -62,6 +62,10 @@
     return dot(left[0], right[0]) + (dot(left[0], right[1]) + dot(left[1], right[0]))
 
 
+def matmul(left, right):
+    return jnp.dot(left, right, preferred_element_type=F32)
+
+
 def times(first, second):
     return (
         first[0] * second[0] - first[1] * second[1],
@@ -77,11 +81,15 @@
     rows, rows_t, lanes, lanes_t = tables
 
     def by_rows(table, pair):
-        out = product(table, split(jnp.concatenate(pair, axis=0)))
+        high, low = split(jnp.concatenate(pair, axis=0))
+        out = matmul(table[0], jnp.concatenate([high, low], axis=1))
+        out = out[:, :size] + (out[:, size:] + matmul(table[1], high))
         return (out[:size], out[size:])
 
     def by_lanes(pair, table):
-        out = product(split(jnp.concatenate(pair, axis=1)), table)
+        high, low = split(jnp.concatenate(pair, axis=1))
+        out = matmul(jnp.concatenate([high, low], axis=0), table[0])
+        out = out[:size] + (out[size:] + matmul(high, table[1]))
         return (out[:, :size], out[:, size:])
 
     mixed = times(by_rows(rows, values), twiddle)
@@ -124,19 +132,15 @@
     def lanes(values, index):
         return jnp.take_along_axis(values, jnp.bitwise_and(index, size - 1), axis=1, mode="promise_in_bounds")
 
+    lower = row * size + lane + jnp.where(leading, shift, shift - 1)
+
     def sample(values):
         below, above = rows_down(values), rows_up(values)
 
-        def displaced(by):
-            source = jnp.where(lane < by, above, jnp.where(lane >= by + size, below, values))
-            return lanes(source, lane + by)
-
-        centre = displaced(shift)
-        return jnp.where(
-            leading,
-            rest * centre + weight * displaced(shift + 1),
-            rest * displaced(shift - 1) + weight * centre,
-        )
+        def window(first):
+            return jnp.where(lane < first, above, jnp.where(lane >= first + size, below, values))
+
+        return rest * lanes(window(shift), lower) + weight * lanes(window(shift + 1), lower + 1)
 
     def spread(values):
         near, far = rest * values, weight * values

time: 69.9 us -> 69.6 us (level)
  no operation moved by 1% of the time
where the time goes in v6:
time: 69.6 us; the launch traced here: 69.4 us
  blocking collectives  33.2 us (48%)
  starting transfers between devices  24.6 us (35%)
  Pallas kernels  5.31 us (8%)
  waiting for transfers between devices  3.19 us (5%)
  between operations  2.62 us (4%)
    all_to_all x1, starting transfers between devices, exchange(): lax.all_to_all(rows[:, None, :], 'tile', 0, 0, axis_index_groups=groups,...  24.6 us
    all_to_all x1, blocking collectives, exchange(): lax.all_to_all(rows[:, None, :], 'tile', 0, 0, axis_index_groups=groups,...  20.1 us
    all_gather x1, blocking collectives, body(): tiles = lax.all_gather(exchange(own), 'dist', axis=0, tiled=True)  8.07 us
    all_gather x2, blocking collectives, of_both_cores(): lax.all_gather(rows, 'dist', axis=0, tiled=True, axis_index_groups=[[0, 1...  5.06 us
    all_to_all x1, waiting for transfers between devices, exchange(): lax.all_to_all(rows[:, None, :], 'tile', 0, 0, axis_index_groups=groups,...  3.19 us
    pallas_call x1, Pallas kernels, run_column(): pl.pallas_call(partial(column_kernel, size), out_shape=jax.ShapeDtypeStru...  2.75 us
    pallas_call x1, Pallas kernels, body(): pl.pallas_call(partial(pack_kernel, size), out_shape=jax.ShapeDtypeStruct...  1.8 us
  transfers between devices with their start and end apart: 1, of which 1 were waited for; matrix products, arithmetic and copies ran while one was open for 1% of the time, Pallas kernels for 0%

profile of v6, /device:TPU:1, one launch (start us, length us, event | category | flops | bytes accessed | tf_op | source)
XLA Modules:
  0.0 69.4 jit_solution(5899172772413821105)
XLA Ops:
  0.6 0.0 copy-start
  0.6 1.8 %pack.1 = f32[256,128]{1,0:T(8,128)} custom-call(f32[128,128]{1,0:T(8,128)} %re_ref.1, f32[128,128]{1,0:T(8,128)} %im_ref.1, f32[128,128]{1,0:T(8,128)} %bitcast.19), custom_call_target="tpu_custom_call" | custom-call | tf_op jit(solution)/shard_map/pack/pallas_call | solution.py:249
  2.5 24.6 %all-to-all-start = ((f32[256,1,128]{2,1,0:T(1,128)}), f32[256,1,128]{2,1,0:T(1,128)S(1)}, u32[]{:S(2)}, u32[]{:S(2)}) async-start(f32[256,1,128]{2,1,0:T(1,128)} %bitcast.16), calls=%async_computation | async-start | bytes 262144 | tf_op jit(solution)/shard_map/all_to_all | solution.py:237
  29.0 0.1 pad_add_fusion.scalars
  29.1 0.3 fusion.7
  29.4 3.2 %all-to-all-done = f32[256,1,128]{2,1,0:T(1,128)S(1)} async-done(((f32[256,1,128]{2,1,0:T(1,128)}), f32[256,1,128]{2,1,0:T(1,128)S(1)}, u32[]{:S(2)}, u32[]{:S(2)}) %all-to-all-start) | async-done | bytes 131104 | tf_op jit(solution)/shard_map/all_to_all | solution.py:237
  32.6 0.0 copy-start.1
  32.6 3.1 %all-gather = f32[512,1,128]{2,0,1:T(8,128)S(1)} all-gather(f32[256,1,128]{2,0,1:T(8,128)S(1)} %bitcast.15), channel_id=2, replica_groups={{0,128},{256,384},{1,129},{257,385},{2,130},{258,386},{3,131},{259,387}..., dimensions={0}, use_global_device_ids=true | all-gather | bytes 393216 | tf_op jit(solution)/shard_map/all_gather | solution.py:242
  35.7 0.0 copy-done
  35.7 0.0 copy-done.1
  35.7 2.7 %column.1 = f32[256,128]{1,0:T(8,128)S(1)} custom-call(s32[2]{0:T(128)S(1)} %pad_add_fusion.scalars, f32[512,128]{1,0:T(8,128)S(1)} %bitcast.13, f32[2,128,128]{2,1,0:T(8,128)S(1)} %maximum_multiply_fusion.phase_ref, bf16[2048,256]{1,0:T(8,128)(2,1)S(1)} %copy-done, f32[2,128,128]{2,1,0:T(8,128)S(1)} %copy-done.1), custom_call_target="tpu_custom_call" | custom-call | tf_op jit(solution)/shard_map/column/pallas_call | solution.py:197
  38.4 2.0 %all_gather.10 = f32[512,128]{1,0:T(8,128)S(1)} all-gather(f32[256,128]{1,0:T(8,128)S(1)} %column.1), channel_id=1, replica_groups={{0,128},{256,384},{1,129},{257,385},{2,130},{258,386},{3,131},{259,387}..., dimensions={0}, use_global_device_ids=true | all-gather | bytes 393216 | tf_op jit(solution)/shard_map/all_gather | solution.py:242
  40.4 20.1 %all_to_all.10 = f32[128,1,128]{2,1,0:T(1,128)S(1)} all-to-all(f32[128,1,128]{2,1,0:T(1,128)S(1)} %bitcast.17), channel_id=1, replica_groups={{104,120,8,24,40,56,72,88,96,112,0,16,32,48,64,80,108,124,12,28,44,60,7..., dimensions={0} | all-to-all | bytes 131072 | tf_op jit(solution)/shard_map/all_to_all | solution.py:237
  60.5 8.1 %all-gather.1 = f32[512,1,128]{2,0,1:T(8,128)S(1)} all-gather(f32[128,1,128]{2,0,1:T(8,128)S(1)} %bitcast.18), channel_id=3, replica_groups=mesh['dist'=4,'tile'=128] {'dist'}, dimensions={0}, use_global_device_ids=true | all-gather | bytes 327680 | tf_op jit(solution)/shard_map/all_gather | solution.py:261
  68.6 0.8 %finish.1 = (f32[128,128]{1,0:T(8,128)}, f32[128,128]{1,0:T(8,128)}) custom-call(f32[512,128]{1,0:T(8,128)S(1)} %bitcast.14), custom_call_target="tpu_custom_call" | custom-call | tf_op jit(solution)/shard_map/finish/pallas_call | solution.py:263
  (3 shorter events, 0.0 us)
Async XLA Ops:
  0.6 35.0 %copy-start = (bf16[2048,256]{1,0:T(8,128)(2,1)S(1)}, bf16[2048,256]{1,0:T(8,128)(2,1)}, u32[]{:S(2)}) copy-start(bf16[2048,256]{1,0:T(8,128)(2,1)} %constant.44.clone.table_ref) | copy-start | bytes 3145732
  2.5 30.1 %all-to-all-start = ((f32[256,1,128]{2,1,0:T(1,128)}), f32[256,1,128]{2,1,0:T(1,128)S(1)}, u32[]{:S(2)}, u32[]{:S(2)}) async-start(f32[256,1,128]{2,1,0:T(1,128)} %bitcast.16), calls=%async_computation | async-start | bytes 262144 | tf_op jit(solution)/shard_map/all_to_all | solution.py:237
  32.6 3.1 %copy-start.1 = (f32[2,128,128]{2,1,0:T(8,128)S(1)}, f32[2,128,128]{2,1,0:T(8,128)}, u32[]{:S(2)}) copy-start(f32[2,128,128]{2,1,0:T(8,128)} %constant.45.clone.twiddle_ref) | copy-start | bytes 393220

commit v7 on v6

--- a/solution.py
+++ b/solution.py
@@ -26,7 +26,7 @@
 
 def layer_slots():
     bits = LAYERS.bit_length() - 1
-    return [int(format(layer ^ LAYERS // 2, f"0{bits}b")[::-1], 2) for layer in range(LAYERS)]
+    return [int(format(layer ^ LAYERS // 2 + 1, f"0{bits}b")[::-1], 2) for layer in range(LAYERS)]
 
 
 def tile_order(size):
@@ -170,7 +170,7 @@
     measured = jnp.where(core_index() == 0, gathered(1), gathered(span + 1))
     wave = propagate((sample(gathered(0)), sample(gathered(span))), tables, twiddle, kernel, size)
     power = wave[0] * wave[0] + wave[1] * wave[1]
-    kept = 1.0 - jnp.sqrt(measured / jnp.maximum(power, 0.01))
+    kept = 1.0 - jnp.sqrt(measured) * lax.rsqrt(jnp.maximum(power, 0.01))
     residual = (kept * wave[0], kept * wave[1])
     back = propagate(residual, tables, twiddle, conj(kernel), size)
     for part in range(2):

time: 69.6 us -> 69.5 us (level)
  waiting for transfers between devices: 3.19 us -> 4.5 us
  blocking collectives: 33.2 us -> 32.3 us
    all_to_all x1, waiting for transfers between devices: 3.19 us -> 4.5 us  [exchange(): lax.all_to_all(rows[:, None, :], 'tile', 0, 0, axis_index_groups=groups,...]
    all_to_all x1, blocking collectives: 20.1 us -> 19.2 us  [exchange(): lax.all_to_all(rows[:, None, :], 'tile', 0, 0, axis_index_groups=groups,...]
    all_gather x2, blocking collectives: 5.06 us -> 4.31 us  [of_both_cores(): lax.all_gather(rows, 'dist', axis=0, tiled=True, axis_index_groups=[[0, 1...]
    all_gather x1, blocking collectives: 8.07 us -> 8.81 us  [body(): tiles = lax.all_gather(exchange(own), 'dist', axis=0, tiled=True)]
where the time goes in v7:
time: 69.5 us; the launch traced here: 69.2 us
  blocking collectives  32.3 us (46%)
  starting transfers between devices  24.1 us (35%)
  Pallas kernels  5.29 us (8%)
  waiting for transfers between devices  4.5 us (6%)
  between operations  2.63 us (4%)
    all_to_all x1, starting transfers between devices, exchange(): lax.all_to_all(rows[:, None, :], 'tile', 0, 0, axis_index_groups=groups,...  24.1 us
    all_to_all x1, blocking collectives, exchange(): lax.all_to_all(rows[:, None, :], 'tile', 0, 0, axis_index_groups=groups,...  19.2 us
    all_gather x1, blocking collectives, body(): tiles = lax.all_gather(exchange(own), 'dist', axis=0, tiled=True)  8.81 us
    all_to_all x1, waiting for transfers between devices, exchange(): lax.all_to_all(rows[:, None, :], 'tile', 0, 0, axis_index_groups=groups,...  4.5 us
    all_gather x2, blocking collectives, of_both_cores(): lax.all_gather(rows, 'dist', axis=0, tiled=True, axis_index_groups=[[0, 1...  4.31 us
    pallas_call x1, Pallas kernels, run_column(): pl.pallas_call(partial(column_kernel, size), out_shape=jax.ShapeDtypeStru...  2.73 us
    pallas_call x1, Pallas kernels, body(): pl.pallas_call(partial(pack_kernel, size), out_shape=jax.ShapeDtypeStruct...  1.8 us
  transfers between devices with their start and end apart: 1, of which 1 were waited for; matrix products, arithmetic and copies ran while one was open for 1% of the time, Pallas kernels for 0%

profile of v7, /device:TPU:1, one launch (start us, length us, event | category | flops | bytes accessed | tf_op | source)
XLA Modules:
  0.0 69.2 jit_solution(5685641776189608453)
XLA Ops:
  0.6 0.0 copy-start
  0.6 1.8 %pack.1 = f32[256,128]{1,0:T(8,128)} custom-call(f32[128,128]{1,0:T(8,128)} %re_ref.1, f32[128,128]{1,0:T(8,128)} %im_ref.1, f32[128,128]{1,0:T(8,128)} %bitcast.19), custom_call_target="tpu_custom_call" | custom-call | tf_op jit(solution)/shard_map/pack/pallas_call | solution.py:249
  2.5 24.1 %all-to-all-start = ((f32[256,1,128]{2,1,0:T(1,128)}), f32[256,1,128]{2,1,0:T(1,128)S(1)}, u32[]{:S(2)}, u32[]{:S(2)}) async-start(f32[256,1,128]{2,1,0:T(1,128)} %bitcast.16), calls=%async_computation | async-start | bytes 262144 | tf_op jit(solution)/shard_map/all_to_all | solution.py:237
  28.5 0.1 pad_add_fusion.scalars
  28.5 0.3 fusion.7
  28.9 4.5 %all-to-all-done = f32[256,1,128]{2,1,0:T(1,128)S(1)} async-done(((f32[256,1,128]{2,1,0:T(1,128)}), f32[256,1,128]{2,1,0:T(1,128)S(1)}, u32[]{:S(2)}, u32[]{:S(2)}) %all-to-all-start) | async-done | bytes 131104 | tf_op jit(solution)/shard_map/all_to_all | solution.py:237
  33.4 0.0 copy-start.1
  33.4 2.3 %all-gather = f32[512,1,128]{2,0,1:T(8,128)S(1)} all-gather(f32[256,1,128]{2,0,1:T(8,128)S(1)} %bitcast.15), channel_id=2, replica_groups={{0,128},{256,384},{1,129},{257,385},{2,130},{258,386},{3,131},{259,387}..., dimensions={0}, use_global_device_ids=true | all-gather | bytes 393216 | tf_op jit(solution)/shard_map/all_gather | solution.py:242
  35.7 0.0 copy-done
  35.7 0.0 copy-done.1
  35.7 2.7 %column.1 = f32[256,128]{1,0:T(8,128)S(1)} custom-call(s32[2]{0:T(128)S(1)} %pad_add_fusion.scalars, f32[512,128]{1,0:T(8,128)S(1)} %bitcast.13, f32[2,128,128]{2,1,0:T(8,128)S(1)} %maximum_multiply_fusion.phase_ref, bf16[2048,256]{1,0:T(8,128)(2,1)S(1)} %copy-done, f32[2,128,128]{2,1,0:T(8,128)S(1)} %copy-done.1), custom_call_target="tpu_custom_call" | custom-call | tf_op jit(solution)/shard_map/column/pallas_call | solution.py:197
  38.4 2.0 %all_gather.10 = f32[512,128]{1,0:T(8,128)S(1)} all-gather(f32[256,128]{1,0:T(8,128)S(1)} %column.1), channel_id=1, replica_groups={{0,128},{256,384},{1,129},{257,385},{2,130},{258,386},{3,131},{259,387}..., dimensions={0}, use_global_device_ids=true | all-gather | bytes 393216 | tf_op jit(solution)/shard_map/all_gather | solution.py:242
  40.5 19.2 %all_to_all.10 = f32[128,1,128]{2,1,0:T(1,128)S(1)} all-to-all(f32[128,1,128]{2,1,0:T(1,128)S(1)} %bitcast.17), channel_id=1, replica_groups={{105,121,9,25,41,57,73,89,97,113,1,17,33,49,65,81,109,125,13,29,45,61,7..., dimensions={0} | all-to-all | bytes 131072 | tf_op jit(solution)/shard_map/all_to_all | solution.py:237
  59.7 8.8 %all-gather.1 = f32[512,1,128]{2,0,1:T(8,128)S(1)} all-gather(f32[128,1,128]{2,0,1:T(8,128)S(1)} %bitcast.18), channel_id=3, replica_groups=mesh['dist'=4,'tile'=128] {'dist'}, dimensions={0}, use_global_device_ids=true | all-gather | bytes 327680 | tf_op jit(solution)/shard_map/all_gather | solution.py:261
  68.5 0.8 %finish.1 = (f32[128,128]{1,0:T(8,128)}, f32[128,128]{1,0:T(8,128)}) custom-call(f32[512,128]{1,0:T(8,128)S(1)} %bitcast.14), custom_call_target="tpu_custom_call" | custom-call | tf_op jit(solution)/shard_map/finish/pallas_call | solution.py:263
  (3 shorter events, 0.0 us)
Async XLA Ops:
  0.6 35.1 %copy-start = (bf16[2048,256]{1,0:T(8,128)(2,1)S(1)}, bf16[2048,256]{1,0:T(8,128)(2,1)}, u32[]{:S(2)}) copy-start(bf16[2048,256]{1,0:T(8,128)(2,1)} %constant.44.clone.table_ref) | copy-start | bytes 3145732
  2.5 30.9 %all-to-all-start = ((f32[256,1,128]{2,1,0:T(1,128)}), f32[256,1,128]{2,1,0:T(1,128)S(1)}, u32[]{:S(2)}, u32[]{:S(2)}) async-start(f32[256,1,128]{2,1,0:T(1,128)} %bitcast.16), calls=%async_computation | async-start | bytes 262144 | tf_op jit(solution)/shard_map/all_to_all | solution.py:237
  33.4 2.3 %copy-start.1 = (f32[2,128,128]{2,1,0:T(8,128)S(1)}, f32[2,128,128]{2,1,0:T(8,128)}, u32[]{:S(2)}) copy-start(f32[2,128,128]{2,1,0:T(8,128)} %constant.45.clone.twiddle_ref) | copy-start | bytes 393220

commit v8 on v7

--- a/solution.py
+++ b/solution.py
@@ -227,9 +227,13 @@
     out_ref[pl.ds(1, size, stride=2), :] = tiles[1].T
 
 
-def finish_kernel(size, tiles_ref, re_ref, im_ref):
-    for part, ref in enumerate((re_ref, im_ref)):
-        ref[...] = (tiles_ref[pl.ds(size * part, size), :] + tiles_ref[pl.ds(size * (part + 2), size), :]).T
+def finish_kernel(size, tiles_ref, re_ref, im_ref, parts, sent):
+    copies = [pltpu.make_async_copy(parts.at[part], ref, sent.at[part]) for part, ref in enumerate((re_ref, im_ref))]
+    for part, copy in enumerate(copies):
+        parts[part] = (tiles_ref[pl.ds(size * part, size), :] + tiles_ref[pl.ds(size * (part + 2), size), :]).T
+        copy.start()
+    for copy in copies:
+        copy.wait()
 
 
 def exchange(rows):
@@ -264,7 +268,8 @@
         partial(finish_kernel, size),
         out_shape=(out, out),
         in_specs=[vmem],
-        out_specs=(vmem, vmem),
+        out_specs=(pl.BlockSpec(memory_space=pl.ANY),) * 2,
+        scratch_shapes=[pltpu.VMEM((2, size, size), F32), pltpu.SemaphoreType.DMA((2,))],
         compiler_params=pltpu.CompilerParams(vmem_limit_bytes=8 * 1024 * 1024),
         name="finish",
     )(tiles)

time: 69.5 us -> 69.5 us (level)
  no operation moved by 1% of the time
where the time goes in v8:
time: 69.5 us; the launch traced here: 69.2 us
  blocking collectives  32.3 us (46%)
  starting transfers between devices  24.1 us (35%)
  Pallas kernels  5.31 us (8%)
  waiting for transfers between devices  4.5 us (6%)
  between operations  2.63 us (4%)
    all_to_all x1, starting transfers between devices, exchange(): lax.all_to_all(rows[:, None, :], 'tile', 0, 0, axis_index_groups=groups,...  24.1 us
    all_to_all x1, blocking collectives, exchange(): lax.all_to_all(rows[:, None, :], 'tile', 0, 0, axis_index_groups=groups,...  19.2 us
    all_gather x1, blocking collectives, body(): tiles = lax.all_gather(exchange(own), 'dist', axis=0, tiled=True)  8.81 us
    all_to_all x1, waiting for transfers between devices, exchange(): lax.all_to_all(rows[:, None, :], 'tile', 0, 0, axis_index_groups=groups,...  4.5 us
    all_gather x2, blocking collectives, of_both_cores(): lax.all_gather(rows, 'dist', axis=0, tiled=True, axis_index_groups=[[0, 1...  4.31 us
    pallas_call x1, Pallas kernels, run_column(): pl.pallas_call(partial(column_kernel, size), out_shape=jax.ShapeDtypeStru...  2.73 us
    pallas_call x1, Pallas kernels, body(): pl.pallas_call(partial(pack_kernel, size), out_shape=jax.ShapeDtypeStruct...  1.8 us
  transfers between devices with their start and end apart: 1, of which 1 were waited for; matrix products, arithmetic and copies ran while one was open for 1% of the time, Pallas kernels for 0%

profile of v8, /device:TPU:1, one launch (start us, length us, event | category | flops | bytes accessed | tf_op | source)
XLA Modules:
  0.0 69.2 jit_solution(2563525244577196411)
XLA Ops:
  0.6 0.0 copy-start
  0.6 1.8 %pack.1 = f32[256,128]{1,0:T(8,128)} custom-call(f32[128,128]{1,0:T(8,128)} %re_ref.1, f32[128,128]{1,0:T(8,128)} %im_ref.1, f32[128,128]{1,0:T(8,128)} %bitcast.19), custom_call_target="tpu_custom_call" | custom-call | tf_op jit(solution)/shard_map/pack/pallas_call | solution.py:253
  2.5 24.1 %all-to-all-start = ((f32[256,1,128]{2,1,0:T(1,128)}), f32[256,1,128]{2,1,0:T(1,128)S(1)}, u32[]{:S(2)}, u32[]{:S(2)}) async-start(f32[256,1,128]{2,1,0:T(1,128)} %bitcast.16), calls=%async_computation | async-start | bytes 262144 | tf_op jit(solution)/shard_map/all_to_all | solution.py:241
  28.5 0.1 pad_add_fusion.scalars
  28.5 0.3 fusion.7
  28.9 4.5 %all-to-all-done = f32[256,1,128]{2,1,0:T(1,128)S(1)} async-done(((f32[256,1,128]{2,1,0:T(1,128)}), f32[256,1,128]{2,1,0:T(1,128)S(1)}, u32[]{:S(2)}, u32[]{:S(2)}) %all-to-all-start) | async-done | bytes 131104 | tf_op jit(solution)/shard_map/all_to_all | solution.py:241
  33.4 0.0 copy-start.1
  33.4 2.3 %all-gather = f32[512,1,128]{2,0,1:T(8,128)S(1)} all-gather(f32[256,1,128]{2,0,1:T(8,128)S(1)} %bitcast.15), channel_id=2, replica_groups={{0,128},{256,384},{1,129},{257,385},{2,130},{258,386},{3,131},{259,387}..., dimensions={0}, use_global_device_ids=true | all-gather | bytes 393216 | tf_op jit(solution)/shard_map/all_gather | solution.py:246
  35.7 0.0 copy-done
  35.7 0.0 copy-done.1
  35.7 2.7 %column.1 = f32[256,128]{1,0:T(8,128)S(1)} custom-call(s32[2]{0:T(128)S(1)} %pad_add_fusion.scalars, f32[512,128]{1,0:T(8,128)S(1)} %bitcast.13, f32[2,128,128]{2,1,0:T(8,128)S(1)} %maximum_multiply_fusion.phase_ref, bf16[2048,256]{1,0:T(8,128)(2,1)S(1)} %copy-done, f32[2,128,128]{2,1,0:T(8,128)S(1)} %copy-done.1), custom_call_target="tpu_custom_call" | custom-call | tf_op jit(solution)/shard_map/column/pallas_call | solution.py:197
  38.4 2.0 %all_gather.10 = f32[512,128]{1,0:T(8,128)S(1)} all-gather(f32[256,128]{1,0:T(8,128)S(1)} %column.1), channel_id=1, replica_groups={{0,128},{256,384},{1,129},{257,385},{2,130},{258,386},{3,131},{259,387}..., dimensions={0}, use_global_device_ids=true | all-gather | bytes 393216 | tf_op jit(solution)/shard_map/all_gather | solution.py:246
  40.5 19.2 %all_to_all.10 = f32[128,1,128]{2,1,0:T(1,128)S(1)} all-to-all(f32[128,1,128]{2,1,0:T(1,128)S(1)} %bitcast.17), channel_id=1, replica_groups={{105,121,9,25,41,57,73,89,97,113,1,17,33,49,65,81,109,125,13,29,45,61,7..., dimensions={0} | all-to-all | bytes 131072 | tf_op jit(solution)/shard_map/all_to_all | solution.py:241
  59.7 8.8 %all-gather.1 = f32[512,1,128]{2,0,1:T(8,128)S(1)} all-gather(f32[128,1,128]{2,0,1:T(8,128)S(1)} %bitcast.18), channel_id=3, replica_groups=mesh['dist'=4,'tile'=128] {'dist'}, dimensions={0}, use_global_device_ids=true | all-gather | bytes 327680 | tf_op jit(solution)/shard_map/all_gather | solution.py:265
  68.5 0.8 %finish.1 = (f32[128,128]{1,0:T(8,128)}, f32[128,128]{1,0:T(8,128)}) custom-call(f32[512,128]{1,0:T(8,128)S(1)} %bitcast.14), custom_call_target="tpu_custom_call" | custom-call | tf_op jit(solution)/shard_map/finish/pallas_call | solution.py:267
  (3 shorter events, 0.0 us)
Async XLA Ops:
  0.6 35.1 %copy-start = (bf16[2048,256]{1,0:T(8,128)(2,1)S(1)}, bf16[2048,256]{1,0:T(8,128)(2,1)}, u32[]{:S(2)}) copy-start(bf16[2048,256]{1,0:T(8,128)(2,1)} %constant.44.clone.table_ref) | copy-start | bytes 3145732
  2.5 30.9 %all-to-all-start = ((f32[256,1,128]{2,1,0:T(1,128)}), f32[256,1,128]{2,1,0:T(1,128)S(1)}, u32[]{:S(2)}, u32[]{:S(2)}) async-start(f32[256,1,128]{2,1,0:T(1,128)} %bitcast.16), calls=%async_computation | async-start | bytes 262144 | tf_op jit(solution)/shard_map/all_to_all | solution.py:241
  33.4 2.3 %copy-start.1 = (f32[2,128,128]{2,1,0:T(8,128)S(1)}, f32[2,128,128]{2,1,0:T(8,128)}, u32[]{:S(2)}) copy-start(f32[2,128,128]{2,1,0:T(8,128)} %constant.45.clone.twiddle_ref) | copy-start | bytes 393220

commit v9 on v7

--- a/solution.py
+++ b/solution.py
@@ -25,8 +25,9 @@
 
 
 def layer_slots():
-    bits = LAYERS.bit_length() - 1
-    return [int(format(layer ^ LAYERS // 2 + 1, f"0{bits}b")[::-1], 2) for layer in range(LAYERS)]
+    near = [0, 15, 14, 13, 12]
+    order = [11, 10, 9, 1, 8, 2, 7, 3, 6, 4, 5] + near
+    return [order.index(layer) for layer in range(LAYERS)]
 
 
 def tile_order(size):

time: 69.5 us -> 69.7 us (level)
  starting transfers between devices: 24.1 us -> 22.4 us
  waiting for transfers between devices: 4.5 us -> 5.53 us
  blocking collectives: 32.3 us -> 33.1 us
    all_to_all x1, starting transfers between devices: 24.1 us -> 22.4 us  [exchange(): lax.all_to_all(rows[:, None, :], 'tile', 0, 0, axis_index_groups=groups,...]
    all_to_all x1, waiting for transfers between devices: 4.5 us -> 5.53 us  [exchange(): lax.all_to_all(rows[:, None, :], 'tile', 0, 0, axis_index_groups=groups,...]
    all_gather x2, blocking collectives: 4.31 us -> 5.15 us  [of_both_cores(): lax.all_gather(rows, 'dist', axis=0, tiled=True, axis_index_groups=[[0, 1...]
    all_gather x1, blocking collectives: 8.81 us -> 8.05 us  [body(): tiles = lax.all_gather(exchange(own), 'dist', axis=0, tiled=True)]
    all_to_all x1, blocking collectives: 19.2 us -> 19.9 us  [exchange(): lax.all_to_all(rows[:, None, :], 'tile', 0, 0, axis_index_groups=groups,...]
where the time goes in v9:
time: 69.7 us; the launch traced here: 69.4 us
  blocking collectives  33.1 us (47%)
  starting transfers between devices  22.4 us (32%)
  waiting for transfers between devices  5.53 us (8%)
  Pallas kernels  5.29 us (8%)
  between operations  2.63 us (4%)
    all_to_all x1, starting transfers between devices, exchange(): lax.all_to_all(rows[:, None, :], 'tile', 0, 0, axis_index_groups=groups,...  22.4 us
    all_to_all x1, blocking collectives, exchange(): lax.all_to_all(rows[:, None, :], 'tile', 0, 0, axis_index_groups=groups,...  19.9 us
    all_gather x1, blocking collectives, body(): tiles = lax.all_gather(exchange(own), 'dist', axis=0, tiled=True)  8.05 us
    all_to_all x1, waiting for transfers between devices, exchange(): lax.all_to_all(rows[:, None, :], 'tile', 0, 0, axis_index_groups=groups,...  5.53 us
    all_gather x2, blocking collectives, of_both_cores(): lax.all_gather(rows, 'dist', axis=0, tiled=True, axis_index_groups=[[0, 1...  5.15 us
    pallas_call x1, Pallas kernels, run_column(): pl.pallas_call(partial(column_kernel, size), out_shape=jax.ShapeDtypeStru...  2.73 us
    pallas_call x1, Pallas kernels, body(): pl.pallas_call(partial(pack_kernel, size), out_shape=jax.ShapeDtypeStruct...  1.8 us
  transfers between devices with their start and end apart: 1, of which 1 were waited for; matrix products, arithmetic and copies ran while one was open for 1% of the time, Pallas kernels for 0%

profile of v9, /device:TPU:1, one launch (start us, length us, event | category | flops | bytes accessed | tf_op | source)
XLA Modules:
  0.0 69.4 jit_solution(16803257305319653368)
XLA Ops:
  0.6 0.0 copy-start
  0.6 1.8 %pack.1 = f32[256,128]{1,0:T(8,128)} custom-call(f32[128,128]{1,0:T(8,128)} %re_ref.1, f32[128,128]{1,0:T(8,128)} %im_ref.1, f32[128,128]{1,0:T(8,128)} %bitcast.19), custom_call_target="tpu_custom_call" | custom-call | tf_op jit(solution)/shard_map/pack/pallas_call | solution.py:250
  2.5 22.4 %all-to-all-start = ((f32[256,1,128]{2,1,0:T(1,128)}), f32[256,1,128]{2,1,0:T(1,128)S(1)}, u32[]{:S(2)}, u32[]{:S(2)}) async-start(f32[256,1,128]{2,1,0:T(1,128)} %bitcast.16), calls=%async_computation | async-start | bytes 262144 | tf_op jit(solution)/shard_map/all_to_all | solution.py:238
  26.8 0.1 pad_add_fusion.scalars
  26.9 0.3 fusion.7
  27.2 5.5 %all-to-all-done = f32[256,1,128]{2,1,0:T(1,128)S(1)} async-done(((f32[256,1,128]{2,1,0:T(1,128)}), f32[256,1,128]{2,1,0:T(1,128)S(1)}, u32[]{:S(2)}, u32[]{:S(2)}) %all-to-all-start) | async-done | bytes 131104 | tf_op jit(solution)/shard_map/all_to_all | solution.py:238
  32.7 0.0 copy-start.1
  32.7 3.2 %all-gather = f32[512,1,128]{2,0,1:T(8,128)S(1)} all-gather(f32[256,1,128]{2,0,1:T(8,128)S(1)} %bitcast.15), channel_id=2, replica_groups={{0,128},{256,384},{1,129},{257,385},{2,130},{258,386},{3,131},{259,387}..., dimensions={0}, use_global_device_ids=true | all-gather | bytes 393216 | tf_op jit(solution)/shard_map/all_gather | solution.py:243
  35.9 0.0 copy-done
  35.9 0.0 copy-done.1
  35.9 2.7 %column.1 = f32[256,128]{1,0:T(8,128)S(1)} custom-call(s32[2]{0:T(128)S(1)} %pad_add_fusion.scalars, f32[512,128]{1,0:T(8,128)S(1)} %bitcast.13, f32[2,128,128]{2,1,0:T(8,128)S(1)} %maximum_multiply_fusion.phase_ref, bf16[2048,256]{1,0:T(8,128)(2,1)S(1)} %copy-done, f32[2,128,128]{2,1,0:T(8,128)S(1)} %copy-done.1), custom_call_target="tpu_custom_call" | custom-call | tf_op jit(solution)/shard_map/column/pallas_call | solution.py:198
  38.6 2.0 %all_gather.10 = f32[512,128]{1,0:T(8,128)S(1)} all-gather(f32[256,128]{1,0:T(8,128)S(1)} %column.1), channel_id=1, replica_groups={{0,128},{256,384},{1,129},{257,385},{2,130},{258,386},{3,131},{259,387}..., dimensions={0}, use_global_device_ids=true | all-gather | bytes 393216 | tf_op jit(solution)/shard_map/all_gather | solution.py:243
  40.7 19.9 %all_to_all.10 = f32[128,1,128]{2,1,0:T(1,128)S(1)} all-to-all(f32[128,1,128]{2,1,0:T(1,128)S(1)} %bitcast.17), channel_id=1, replica_groups={{107,123,11,27,43,59,75,91,106,122,10,26,42,58,74,90,105,121,9,25,41,57..., dimensions={0} | all-to-all | bytes 131072 | tf_op jit(solution)/shard_map/all_to_all | solution.py:238
  60.6 8.1 %all-gather.1 = f32[512,1,128]{2,0,1:T(8,128)S(1)} all-gather(f32[128,1,128]{2,0,1:T(8,128)S(1)} %bitcast.18), channel_id=3, replica_groups=mesh['dist'=4,'tile'=128] {'dist'}, dimensions={0}, use_global_device_ids=true | all-gather | bytes 327680 | tf_op jit(solution)/shard_map/all_gather | solution.py:262
  68.6 0.8 %finish.1 = (f32[128,128]{1,0:T(8,128)}, f32[128,128]{1,0:T(8,128)}) custom-call(f32[512,128]{1,0:T(8,128)S(1)} %bitcast.14), custom_call_target="tpu_custom_call" | custom-call | tf_op jit(solution)/shard_map/finish/pallas_call | solution.py:264
  (3 shorter events, 0.0 us)
Async XLA Ops:
  0.6 35.3 %copy-start = (bf16[2048,256]{1,0:T(8,128)(2,1)S(1)}, bf16[2048,256]{1,0:T(8,128)(2,1)}, u32[]{:S(2)}) copy-start(bf16[2048,256]{1,0:T(8,128)(2,1)} %constant.44.clone.table_ref) | copy-start | bytes 3145732
  2.5 30.3 %all-to-all-start = ((f32[256,1,128]{2,1,0:T(1,128)}), f32[256,1,128]{2,1,0:T(1,128)S(1)}, u32[]{:S(2)}, u32[]{:S(2)}) async-start(f32[256,1,128]{2,1,0:T(1,128)} %bitcast.16), calls=%async_computation | async-start | bytes 262144 | tf_op jit(solution)/shard_map/all_to_all | solution.py:238
  32.7 3.2 %copy-start.1 = (f32[2,128,128]{2,1,0:T(8,128)S(1)}, f32[2,128,128]{2,1,0:T(8,128)}, u32[]{:S(2)}) copy-start(f32[2,128,128]{2,1,0:T(8,128)} %constant.45.clone.twiddle_ref) | copy-start | bytes 393220

commit v10 on v9

--- a/solution.py
+++ b/solution.py
@@ -26,7 +26,7 @@
 
 def layer_slots():
     near = [0, 15, 14, 13, 12]
-    order = [11, 10, 9, 1, 8, 2, 7, 3, 6, 4, 5] + near
+    order = [10, 9, 1, 8, 2, 7, 3, 6, 4, 5] + near + [11]
     return [order.index(layer) for layer in range(LAYERS)]
 
 

time: 69.7 us -> 69.6 us (level)
  starting transfers between devices: 22.4 us -> 23.2 us
    all_to_all x1, starting transfers between devices: 22.4 us -> 23.2 us  [exchange(): lax.all_to_all(rows[:, None, :], 'tile', 0, 0, axis_index_groups=groups,...]
where the time goes in v10:
time: 69.6 us; the launch traced here: 69.4 us
  blocking collectives  32.6 us (47%)
  starting transfers between devices  23.2 us (33%)
  Pallas kernels  5.29 us (8%)
  waiting for transfers between devices  5.24 us (8%)
  between operations  2.63 us (4%)
    all_to_all x1, starting transfers between devices, exchange(): lax.all_to_all(rows[:, None, :], 'tile', 0, 0, axis_index_groups=groups,...  23.2 us
    all_to_all x1, blocking collectives, exchange(): lax.all_to_all(rows[:, None, :], 'tile', 0, 0, axis_index_groups=groups,...  19.8 us
    all_gather x1, blocking collectives, body(): tiles = lax.all_gather(exchange(own), 'dist', axis=0, tiled=True)  8.14 us
    all_to_all x1, waiting for transfers between devices, exchange(): lax.all_to_all(rows[:, None, :], 'tile', 0, 0, axis_index_groups=groups,...  5.24 us
    all_gather x2, blocking collectives, of_both_cores(): lax.all_gather(rows, 'dist', axis=0, tiled=True, axis_index_groups=[[0, 1...  4.58 us
    pallas_call x1, Pallas kernels, run_column(): pl.pallas_call(partial(column_kernel, size), out_shape=jax.ShapeDtypeStru...  2.73 us
    pallas_call x1, Pallas kernels, body(): pl.pallas_call(partial(pack_kernel, size), out_shape=jax.ShapeDtypeStruct...  1.8 us
  transfers between devices with their start and end apart: 1, of which 1 were waited for; matrix products, arithmetic and copies ran while one was open for 1% of the time, Pallas kernels for 0%

profile of v10, /device:TPU:1, one launch (start us, length us, event | category | flops | bytes accessed | tf_op | source)
XLA Modules:
  0.0 69.4 jit_solution(6456448956886523018)
XLA Ops:
  0.6 0.0 copy-start
  0.6 1.8 %pack.1 = f32[256,128]{1,0:T(8,128)} custom-call(f32[128,128]{1,0:T(8,128)} %re_ref.1, f32[128,128]{1,0:T(8,128)} %im_ref.1, f32[128,128]{1,0:T(8,128)} %bitcast.19), custom_call_target="tpu_custom_call" | custom-call | tf_op jit(solution)/shard_map/pack/pallas_call | solution.py:250
  2.5 23.2 %all-to-all-start = ((f32[256,1,128]{2,1,0:T(1,128)}), f32[256,1,128]{2,1,0:T(1,128)S(1)}, u32[]{:S(2)}, u32[]{:S(2)}) async-start(f32[256,1,128]{2,1,0:T(1,128)} %bitcast.16), calls=%async_computation | async-start | bytes 262144 | tf_op jit(solution)/shard_map/all_to_all | solution.py:238
  27.6 0.1 pad_add_fusion.scalars
  27.7 0.3 fusion.7
  28.0 5.2 %all-to-all-done = f32[256,1,128]{2,1,0:T(1,128)S(1)} async-done(((f32[256,1,128]{2,1,0:T(1,128)}), f32[256,1,128]{2,1,0:T(1,128)S(1)}, u32[]{:S(2)}, u32[]{:S(2)}) %all-to-all-start) | async-done | bytes 131104 | tf_op jit(solution)/shard_map/all_to_all | solution.py:238
  33.3 0.0 copy-start.1
  33.3 2.6 %all-gather = f32[512,1,128]{2,0,1:T(8,128)S(1)} all-gather(f32[256,1,128]{2,0,1:T(8,128)S(1)} %bitcast.15), channel_id=2, replica_groups={{0,128},{256,384},{1,129},{257,385},{2,130},{258,386},{3,131},{259,387}..., dimensions={0}, use_global_device_ids=true | all-gather | bytes 393216 | tf_op jit(solution)/shard_map/all_gather | solution.py:243
  35.9 0.0 copy-done
  35.9 0.0 copy-done.1
  35.9 2.7 %column.1 = f32[256,128]{1,0:T(8,128)S(1)} custom-call(s32[2]{0:T(128)S(1)} %pad_add_fusion.scalars, f32[512,128]{1,0:T(8,128)S(1)} %bitcast.13, f32[2,128,128]{2,1,0:T(8,128)S(1)} %maximum_multiply_fusion.phase_ref, bf16[2048,256]{1,0:T(8,128)(2,1)S(1)} %copy-done, f32[2,128,128]{2,1,0:T(8,128)S(1)} %copy-done.1), custom_call_target="tpu_custom_call" | custom-call | tf_op jit(solution)/shard_map/column/pallas_call | solution.py:198
  38.6 2.0 %all_gather.10 = f32[512,128]{1,0:T(8,128)S(1)} all-gather(f32[256,128]{1,0:T(8,128)S(1)} %column.1), channel_id=1, replica_groups={{0,128},{256,384},{1,129},{257,385},{2,130},{258,386},{3,131},{259,387}..., dimensions={0}, use_global_device_ids=true | all-gather | bytes 393216 | tf_op jit(solution)/shard_map/all_gather | solution.py:243
  40.6 19.8 %all_to_all.10 = f32[128,1,128]{2,1,0:T(1,128)S(1)} all-to-all(f32[128,1,128]{2,1,0:T(1,128)S(1)} %bitcast.17), channel_id=1, replica_groups={{106,122,10,26,42,58,74,90,105,121,9,25,41,57,73,89,97,113,1,17,33,49,6..., dimensions={0} | all-to-all | bytes 131072 | tf_op jit(solution)/shard_map/all_to_all | solution.py:238
  60.5 8.1 %all-gather.1 = f32[512,1,128]{2,0,1:T(8,128)S(1)} all-gather(f32[128,1,128]{2,0,1:T(8,128)S(1)} %bitcast.18), channel_id=3, replica_groups=mesh['dist'=4,'tile'=128] {'dist'}, dimensions={0}, use_global_device_ids=true | all-gather | bytes 327680 | tf_op jit(solution)/shard_map/all_gather | solution.py:262
  68.6 0.8 %finish.1 = (f32[128,128]{1,0:T(8,128)}, f32[128,128]{1,0:T(8,128)}) custom-call(f32[512,128]{1,0:T(8,128)S(1)} %bitcast.14), custom_call_target="tpu_custom_call" | custom-call | tf_op jit(solution)/shard_map/finish/pallas_call | solution.py:264
  (3 shorter events, 0.0 us)
Async XLA Ops:
  0.6 35.2 %copy-start = (bf16[2048,256]{1,0:T(8,128)(2,1)S(1)}, bf16[2048,256]{1,0:T(8,128)(2,1)}, u32[]{:S(2)}) copy-start(bf16[2048,256]{1,0:T(8,128)(2,1)} %constant.44.clone.table_ref) | copy-start | bytes 3145732
  2.5 30.8 %all-to-all-start = ((f32[256,1,128]{2,1,0:T(1,128)}), f32[256,1,128]{2,1,0:T(1,128)S(1)}, u32[]{:S(2)}, u32[]{:S(2)}) async-start(f32[256,1,128]{2,1,0:T(1,128)} %bitcast.16), calls=%async_computation | async-start | bytes 262144 | tf_op jit(solution)/shard_map/all_to_all | solution.py:238
  33.3 2.6 %copy-start.1 = (f32[2,128,128]{2,1,0:T(8,128)S(1)}, f32[2,128,128]{2,1,0:T(8,128)}, u32[]{:S(2)}) copy-start(f32[2,128,128]{2,1,0:T(8,128)} %constant.45.clone.twiddle_ref) | copy-start | bytes 393220
